TPU v7x, 1024 devices: a whole 4x8x16 slice. The times are simulated.
1024 devices in a mesh: shard: 64 (over y, x, core), rep: 16 (over z).
Axes of the slice: x: 4, y: 8, z: 16, core: 2. Of those that a mesh axis runs over, the one named last changes fastest.
Arguments:
- table_a: bfloat16 [65536, 64], P('shard'), may hold values from -6 to 6
- table_b: bfloat16 [65536, 32], P('shard'), may hold values from -6 to 6
- proj_a: bfloat16 [64, 256], replicated, may hold values from -0.75 to 0.75
- proj_b: bfloat16 [32, 256], replicated, may hold values from -1 to 1
- owner_a: int32 [1048576, 1], P(('shard', 'rep')), may hold values from 0 to 63; in each aligned block of 1024 rows (0 to 1023, 1024 to 2047, ...) at most 24 rows name the same one
- row_a: int32 [1048576], P(('shard', 'rep')), may hold values from 0 to 1023
- bag_a: int32 [1024, 1024], P(('shard', 'rep')), may hold values from 0 to 511, never falling along the last dimension, each value on 1 to 4 neighbouring positions
- owner_b: int32 [1048576, 1], P(('shard', 'rep')), may hold values from 0 to 63; in each aligned block of 1024 rows (0 to 1023, 1024 to 2047, ...) at most 24 rows name the same one
- row_b: int32 [1048576], P(('shard', 'rep')), may hold values from 0 to 1023
- bag_b: int32 [1024, 1024], P(('shard', 'rep')), may hold values from 0 to 511, never falling along the last dimension, each value on 1 to 4 neighbouring positions
- d_pooled: bfloat16 [524288, 256], P(('shard', 'rep')), may hold values from -6 to 6
Outputs:
- pooled: bfloat16 [524288, 256], P(('shard', 'rep'))
- grad_table_a: float32 [65536, 64], P('shard')
- grad_table_b: float32 [65536, 32], P('shard')
- grad_proj_a: float32 [64, 256], replicated
- grad_proj_b: float32 [32, 256], replicated
Inputs may be any that keep to these rules, and one draw needn't show every extreme that they name: `owner_a`: among the lookups of one device, at most 24 name the same owner; some owner is named by exactly 24. `owner_b`: among the lookups of one device, at most 24 name the same owner; some owner is named by exactly 24. `bag_a`: along each device's row the bag never falls; every bag has 1 to 4 lookups, some exactly 4. `bag_b`: along each device's row the bag never falls; every bag has 1 to 4 lookups, some exactly 4.
All inputs are finite; a program needn't handle non-finite values.
Results may differ from a plain program's by a relative error of at most 0.0065.
Values may be sent and summed in bfloat16 or wider, within the bound.
A program may use at most 32 MiB of HBM per device.

v0:
```python
import jax
import jax.numpy as jnp
from jax import lax
from jax.sharding import PartitionSpec as P


def slot_positions(owner, shards):
    owners = owner[:, 0]
    member = (owners[:, None] == jnp.arange(shards, dtype=jnp.int32)[None, :]).astype(jnp.int32)
    position = jnp.sum(jnp.cumsum(member, axis=0) * member, axis=1) - 1
    return (owners, position)


def lift_rows(gathered, proj):
    return jnp.einsum("scw,we->sce", gathered, proj, preferred_element_type=jnp.float32).astype(
        jnp.bfloat16
    )


def bag_onehot(bag, bag_count):
    return (bag[0][None, :] == jnp.arange(bag_count, dtype=jnp.int32)[:, None]).astype(jnp.bfloat16)


def body(table_a, table_b, proj_a, proj_b, owner_a, row_a, bag_a, owner_b, row_b, bag_b, d_pooled):
    shards = lax.axis_size("shard")
    replicas = lax.axis_size("rep")
    lookups = row_a.shape[0]
    capacity = 3 * lookups // (2 * shards)
    bag_count = d_pooled.shape[0]
    owners_a, position_a = slot_positions(owner_a, shards)
    owners_b, position_b = slot_positions(owner_b, shards)
    request_a = jnp.zeros((shards, capacity), jnp.int32).at[owners_a, position_a].set(row_a)
    request_b = jnp.zeros((shards, capacity), jnp.int32).at[owners_b, position_b].set(row_b)
    wanted_a, wanted_b = (
        lax.all_to_all(request_a, "shard", split_axis=0, concat_axis=0, tiled=True),
        lax.all_to_all(request_b, "shard", split_axis=0, concat_axis=0, tiled=True),
    )
    fetched_a = table_a[wanted_a]
    fetched_b = table_b[wanted_b]
    onehot_a = bag_onehot(bag_a, bag_count)
    onehot_b = bag_onehot(bag_b, bag_count)
    lift_grad_a = jnp.einsum(
        "bl,be->le", onehot_a, d_pooled, preferred_element_type=jnp.float32
    ).astype(jnp.bfloat16)
    lift_grad_b = jnp.einsum(
        "bl,be->le", onehot_b, d_pooled, preferred_element_type=jnp.float32
    ).astype(jnp.bfloat16)
    embed = d_pooled.shape[1]
    slots_a, slots_b = (
        lax.all_to_all(
            lift_rows(fetched_a, proj_a), "shard", split_axis=0, concat_axis=0, tiled=True
        ),
        lax.all_to_all(
            lift_rows(fetched_b, proj_b), "shard", split_axis=0, concat_axis=0, tiled=True
        ),
    )
    lifted_a = slots_a[owners_a, position_a]
    lifted_b = slots_b[owners_b, position_b]
    buffer_a = (
        jnp.zeros((shards, capacity, embed), jnp.bfloat16).at[owners_a, position_a].set(lift_grad_a)
    )
    buffer_b = (
        jnp.zeros((shards, capacity, embed), jnp.bfloat16).at[owners_b, position_b].set(lift_grad_b)
    )
    back_a, back_b = (
        lax.all_to_all(buffer_a, "shard", split_axis=0, concat_axis=0, tiled=True),
        lax.all_to_all(buffer_b, "shard", split_axis=0, concat_axis=0, tiled=True),
    )
    row_grad_a = jnp.einsum(
        "sce,we->scw", back_a, proj_a, preferred_element_type=jnp.float32
    ).astype(jnp.bfloat16)
    row_grad_b = jnp.einsum(
        "sce,we->scw", back_b, proj_b, preferred_element_type=jnp.float32
    ).astype(jnp.bfloat16)
    partial_a = jnp.einsum("scw,sce->we", fetched_a, back_a, preferred_element_type=jnp.float32)
    partial_b = jnp.einsum("scw,sce->we", fetched_b, back_b, preferred_element_type=jnp.float32)
    pooled = jnp.dot(onehot_a, lifted_a, preferred_element_type=jnp.float32)
    pooled = (pooled + jnp.dot(onehot_b, lifted_b, preferred_element_type=jnp.float32)).astype(
        jnp.bfloat16
    )
    local_a = jnp.zeros(table_a.shape, jnp.float32).at[wanted_a].add(row_grad_a.astype(jnp.float32))
    local_b = jnp.zeros(table_b.shape, jnp.float32).at[wanted_b].add(row_grad_b.astype(jnp.float32))
    grad_table_a, grad_table_b = lax.psum((local_a, local_b), "rep")
    summed_a, summed_b = lax.psum((partial_a, partial_b), ("shard", "rep"))
    grad_scale = 1.0 / jnp.sqrt(jnp.float32(lookups * shards * replicas))
    return (pooled, grad_table_a, grad_table_b, summed_a * grad_scale, summed_b * grad_scale)


def solution(mesh):
    in_specs = (
        P("shard", None),
        P("shard", None),
        P(),
        P(),
        P(("shard", "rep"), None),
        P(("shard", "rep")),
        P(("shard", "rep"), None),
        P(("shard", "rep"), None),
        P(("shard", "rep")),
        P(("shard", "rep"), None),
        P(("shard", "rep"), None),
    )
    out_specs = (P(("shard", "rep"), None), P("shard", None), P("shard", None), P(), P())
    return jax.shard_map(body, mesh=mesh, in_specs=in_specs, out_specs=out_specs, check_vma=False)
```

profile of v0, /device:TPU:1, one launch (start us, length us, event | category | flops | bytes accessed | tf_op | source)
XLA Modules:
  0.0 796.8 jit_solution(16864280886887094542)
XLA Ops:
  7.9 18.0 %reduce-window.16 = s32[64,8,128]{2,1,0:T(8,128)S(1)} reduce-window(s32[64,8,128]{2,1,0:T(8,128)S(1)} %fusion.27, s32[]{:T(128)} %constant.9.clone.1), window={size=1x1x128 pad=0_0x0_0x127_0}, to_apply=%region_4.5 | reduce-window | flops 8323072 | bytes 524292 | tf_op jit(solution)/shard_map/reduce-window.2
  26.7 18.0 %reduce-window.14 = s32[64,8,128]{2,1,0:T(8,128)S(1)} reduce-window(s32[64,8,128]{2,1,0:T(8,128)S(1)} %fusion.26, s32[]{:T(128)} %constant.9.clone.1), window={size=1x1x128 pad=0_0x0_0x127_0}, to_apply=%region_0.0 | reduce-window | flops 8323072 | bytes 524292 | tf_op jit(solution)/shard_map/reduce-window
  45.7 4.5 scatter_custom_fusion.3
  51.0 18.2 %all-to-all-start.2 = ((s32[64,1,24]{2,1,0:T(1,128)}), s32[64,1,24]{2,1,0:T(1,128)S(1)}, u32[]{:S(2)}, u32[]{:S(2)}) async-start(s32[64,1,24]{2,1,0:T(1,128)} %copy.52), calls=%async_computation.2 | async-start | bytes 65536 | tf_op jit(solution)/shard_map/all_to_all | solution.py:36
  69.2 4.5 scatter_custom_fusion.2
  74.4 4.2 all-to-all-done.2
  78.6 6.3 all-to-all-start
  85.6 5.9 scatter_custom_fusion.4
  94.2 7.8 all-to-all-start.4
  102.7 5.9 scatter_custom_fusion.5
  108.6 16.1 %all-to-all-done.4 = bf16[64,24,256]{2,1,0:T(8,128)(2,1)S(1)} async-done(((bf16[64,24,256]{2,1,0:T(8,128)(2,1)}), bf16[64,24,256]{2,1,0:T(8,128)(2,1)S(1)}, u32[]{:S(2)}, u32[]{:S(2)}) %all-to-all-start.4) | async-done | bytes 786464 | tf_op jit(solution)/shard_map/all_to_all | solution.py:66
  124.7 6.4 all-to-all-start.5
  135.9 18.0 %all-to-all-done.5 = bf16[64,24,256]{2,1,0:T(8,128)(2,1)S(1)} async-done(((bf16[64,24,256]{2,1,0:T(8,128)(2,1)}), bf16[64,24,256]{2,1,0:T(8,128)(2,1)S(1)}, u32[]{:S(2)}, u32[]{:S(2)}) %all-to-all-start.5) | async-done | bytes 786464 | tf_op jit(solution)/shard_map/all_to_all | solution.py:67
  153.8 6.2 all-to-all-start.3
  160.4 3.2 gather_fusion
  164.9 18.0 %all-to-all-done.3 = bf16[64,24,256]{2,1,0:T(8,128)(2,1)S(1)} async-done(((bf16[64,24,256]{2,1,0:T(8,128)(2,1)}), bf16[64,24,256]{2,1,0:T(8,128)(2,1)S(1)}, u32[]{:S(2)}, u32[]{:S(2)}) %all-to-all-start.3) | async-done | bytes 786464 | tf_op jit(solution)/shard_map/all_to_all | solution.py:53
  182.8 6.2 all-to-all-start.1
  193.2 9.6 %scatter_custom_fusion = f32[1024,64]{1,0:T(8,128)} fusion(s32[1536]{0:T(1024)S(1)} %reshape.162, bf16[1536,64]{1,0:T(8,128)(2,1)S(1)} %bitcast.97, f32[]{:T(128)} %constant.27.clone.1), kind=kCustom, calls=%fused_computation.32 | custom fusion | flops 196608 | bytes 655364 | tf_op jit(solution)/shard_map/scatter-add | solution.py:81
  202.8 9.6 %scatter_custom_fusion.1 = f32[1024,32]{1,0:T(8,128)} fusion(s32[1536]{0:T(1024)S(1)} %reshape.176, bf16[1536,32]{1,0:T(8,128)(2,1)S(1)} %bitcast.96, f32[]{:T(128)} %constant.27.clone.1), kind=kCustom, calls=%fused_computation.30 | custom fusion | flops 98304 | bytes 524292 | tf_op jit(solution)/shard_map/scatter-add | solution.py:82
  212.7 130.7 %psum.31 = f32[32,256]{1,0:T(8,128)S(1)} all-reduce(f32[32,256]{1,0:T(8,128)S(1)} %convolution_bitcast_fusion.1), channel_id=1, replica_groups=mesh['shard'=64,'rep'=16] {'shard','rep'}, use_global_device_ids=true, to_apply=%region_15.16 | all-reduce | flops 8192 | bytes 65536 | tf_op jit(solution)/shard_map/psum | solution.py:84
  344.0 5.8 gather_fusion.3
  350.3 5.8 gather_fusion.1
  357.3 300.7 %all-reduce.4.cloned.1.call-done = f32[64,256]{1,0:T(8,128)} async-done(((f32[64,256]{1,0:T(8,128)}), f32[64,256]{1,0:T(8,128)}) %all-reduce.4.cloned.1.call-update) | async-done | bytes 65552 | tf_op jit(solution)/shard_map/psum | solution.py:84
  659.4 127.8 %all-reduce.6.cloned.1.call-done = (f32[1024,64]{1,0:T(8,128)}, f32[1024,32]{1,0:T(8,128)}) async-done(((f32[1024,64]{1,0:T(8,128)}, f32[1024,32]{1,0:T(8,128)}), (f32[1024,64]{1,0:T(8,128)}, f32[1024,32]{1,0:T(8,128)})) %all-reduce.6.cloned.1.call-update) | async-done | bytes 393232 | tf_op jit(solution)/shard_map/psum | solution.py:83
  (90 shorter events, 25.2 us)
Async XLA Ops:
  7.2 77.7 %copy-start = (bf16[512,256]{1,0:T(8,128)(2,1)S(1)}, bf16[512,256]{1,0:T(8,128)(2,1)}, u32[]{:S(2)}) copy-start(bf16[512,256]{1,0:T(8,128)(2,1)} %param.21) | copy-start | bytes 786436
  25.9 0.8 copy-start.11
  44.8 0.7 copy-start.14
  44.8 0.8 copy-start.12
  44.8 0.8 copy-start.13
  44.9 40.0 %copy-start.16 = (s32[1,1024]{1,0:T(1,128)S(1)}, s32[1,1024]{1,0:T(1,128)}, u32[]{:S(2)}) copy-start(s32[1,1024]{1,0:T(1,128)} %param.17) | copy-start | bytes 12292
  51.0 27.6 %all-to-all-start.2 = ((s32[64,1,24]{2,1,0:T(1,128)}), s32[64,1,24]{2,1,0:T(1,128)S(1)}, u32[]{:S(2)}, u32[]{:S(2)}) async-start(s32[64,1,24]{2,1,0:T(1,128)} %copy.52), calls=%async_computation.2 | async-start | bytes 65536 | tf_op jit(solution)/shard_map/all_to_all | solution.py:36
  78.6 15.6 %all-to-all-start = ((s32[64,1,24]{2,1,0:T(1,128)}), s32[64,1,24]{2,1,0:T(1,128)S(1)}, u32[]{:S(2)}, u32[]{:S(2)}) async-start(s32[64,1,24]{2,1,0:T(1,128)} %copy.48), calls=%async_computation | async-start | bytes 65536 | tf_op jit(solution)/shard_map/all_to_all | solution.py:35
  94.2 7.8 copy-start.15
  94.2 30.5 %all-to-all-start.4 = ((bf16[64,24,256]{2,1,0:T(8,128)(2,1)}), bf16[64,24,256]{2,1,0:T(8,128)(2,1)S(1)}, u32[]{:S(2)}, u32[]{:S(2)}) async-start(bf16[64,24,256]{2,1,0:T(8,128)(2,1)} %bitcast.26), calls=%async_computation.4 | async-start | bytes 1572864 | tf_op jit(solution)/shard_map/all_to_all | solution.py:66
  124.7 6.4 copy-start.9
  124.7 29.1 %all-to-all-start.5 = ((bf16[64,24,256]{2,1,0:T(8,128)(2,1)}), bf16[64,24,256]{2,1,0:T(8,128)(2,1)S(1)}, u32[]{:S(2)}, u32[]{:S(2)}) async-start(bf16[64,24,256]{2,1,0:T(8,128)(2,1)} %bitcast.28), calls=%async_computation.5 | async-start | bytes 1572864 | tf_op jit(solution)/shard_map/all_to_all | solution.py:67
  131.4 3.2 copy-start.8
  134.6 19.2 %copy-start.2 = (bf16[1536,32]{1,0:T(8,128)(2,1)}, bf16[1536,32]{1,0:T(8,128)(2,1)S(1)}, u32[]{:S(2)}) copy-start(bf16[1536,32]{1,0:T(8,128)(2,1)S(1)} %gather_fusion.2) | copy-start | bytes 294916
  135.9 24.2 %copy-start.6 = (bf16[1024,64]{0,1:T(8,128)(2,1)S(1)}, bf16[1024,64]{0,1:T(8,128)(2,1)}, u32[]{:S(2)}) copy-start(bf16[1024,64]{0,1:T(8,128)(2,1)} %param.11) | copy-start | bytes 393220
  153.8 29.0 %all-to-all-start.3 = ((bf16[64,24,256]{2,1,0:T(8,128)(2,1)}), bf16[64,24,256]{2,1,0:T(8,128)(2,1)S(1)}, u32[]{:S(2)}, u32[]{:S(2)}) async-start(bf16[64,24,256]{2,1,0:T(8,128)(2,1)} %convolution_convert_fusion), calls=%async_computation.3 | async-start | bytes 1572864 | tf_op jit(solution)/shard_map/all_to_all | solution.py:53
  160.4 3.2 copy-start.7
  163.6 19.2 %copy-start.1 = (bf16[1536,64]{1,0:T(8,128)(2,1)}, bf16[1536,64]{1,0:T(8,128)(2,1)S(1)}, u32[]{:S(2)}) copy-start(bf16[1536,64]{1,0:T(8,128)(2,1)S(1)} %gather_fusion) | copy-start | bytes 589828
  182.8 167.4 %all-to-all-start.1 = ((bf16[64,24,256]{2,1,0:T(8,128)(2,1)}), bf16[64,24,256]{2,1,0:T(8,128)(2,1)S(1)}, u32[]{:S(2)}, u32[]{:S(2)}) async-start(bf16[64,24,256]{2,1,0:T(8,128)(2,1)} %convolution_convert_fusion.1), calls=%async_computation.1 | async-start | bytes 1572864 | tf_op jit(solution)/shard_map/all_to_all | solution.py:50
  189.1 468.9 %all-reduce.4.cloned.1.call-start = ((), (), s32[]{:S(2)}) async-start(), calls=%async_computation.6 | async-start | bytes 131072 | tf_op jit(solution)/shard_map/psum | solution.py:84
  191.1 596.1 %all-reduce.6.cloned.1.call-start = ((), (), s32[]{:S(2)}) async-start(), calls=%async_computation.7 | async-start | bytes 2097152 | tf_op jit(solution)/shard_map/psum | solution.py:83
  192.2 1.0 copy-start.4
  202.8 9.6 %copy-start.3 = (bf16[1536,32]{1,0:T(8,128)(2,1)S(1)}, bf16[1536,32]{1,0:T(8,128)(2,1)}, u32[]{:S(2)}) copy-start(bf16[1536,32]{1,0:T(8,128)(2,1)} %copy-done.2) | copy-start | bytes 294916
  787.2 2.0 copy-start.5
  (1 other events, 0.7 us)
Sparse Core Ops, SparseCore 0:
  196.0 461.9 all-reduce.3
  660.3 126.8 all-reduce.5
where the time goes:
time: 807 us; the launch traced here: 797 us
  waiting for transfers between devices  487 us (60%)
  blocking collectives  131 us (16%)
  other arithmetic  58.8 us (7%)
  starting transfers between devices  51.2 us (6%)
  local copies, waits for them, and re-layouts  45.2 us (6%)
  between operations  14.5 us (2%)
  matrix products  9.19 us (1%)
    psum x1, waiting for transfers between devices, body(): summed_a, summed_b = lax.psum((partial_a, partial_b), ('shard', 'rep'))  301 us
    psum x1, blocking collectives, body(): summed_a, summed_b = lax.psum((partial_a, partial_b), ('shard', 'rep'))  131 us
    psum x1, waiting for transfers between devices, body(): grad_table_a, grad_table_b = lax.psum((local_a, local_b), 'rep')  128 us
    another operation x6, other arithmetic  36.4 us
    unnamed x44, local copies, waits for them, and re-layouts  24.9 us
    all_to_all x1, starting transfers between devices, body(): lax.all_to_all(request_b, 'shard', split_axis=0, concat_axis=0, tiled=True)  18.2 us
    all_to_all x1, waiting for transfers between devices, body(): lax.all_to_all(lift_rows(fetched_b, proj_b), 'shard', split_axis=0, conca...  18 us
    all_to_all x1, waiting for transfers between devices, body(): lax.all_to_all(buffer_b, 'shard', split_axis=0, concat_axis=0, tiled=True)  18 us
  transfers between devices with their start and end apart: 8, of which 7 were waited for; matrix products, arithmetic and copies ran while one was open for 8% of the time, Pallas kernels for 0%

commit v1 on v0

v1 whole, which is shorter than its diff:
```python
import jax
import jax.numpy as jnp
from jax import lax
from jax.sharding import PartitionSpec as P

F32, BF16 = jnp.float32, jnp.bfloat16
BASE = 32


def dot(left, right, dims):
    return lax.dot_general(left, right, (dims, ((), ())), preferred_element_type=F32)


def slot_of(owner, shards, capacity):
    lookups = owner.shape[1]
    named = owner == lax.broadcasted_iota(jnp.int32, (shards, lookups), 0)
    before = lax.broadcasted_iota(jnp.int32, (lookups, lookups), 0) < lax.broadcasted_iota(
        jnp.int32, (lookups, lookups), 1
    )
    earlier = dot(named.astype(BF16), before.astype(BF16), ((1,), (0,)))
    position = jnp.sum(jnp.where(named, earlier, 0.0), axis=0, keepdims=True)
    return owner * capacity + position.astype(jnp.int32)


def onehot_rows(index, count):
    shape = (count, index.shape[1])
    return (index == lax.broadcasted_iota(jnp.int32, shape, 0)).astype(BF16)


def onehot_columns(index, count):
    shape = (index.shape[0], count)
    return (index == lax.broadcasted_iota(jnp.int32, shape, 1)).astype(BF16)


def exchange(x, axis):
    return lax.all_to_all(x, axis, split_axis=0, concat_axis=0, tiled=True)


def spread(x, axis):
    return exchange(jnp.broadcast_to(x[None], (lax.axis_size(axis),) + x.shape), axis)


def body(table_a, table_b, proj_a, proj_b, owner_a, row_a, bag_a, owner_b, row_b, bag_b, d_pooled):
    shards = lax.axis_size("shard")
    replicas = lax.axis_size("rep")
    lookups = row_a.shape[0]
    rows, wide_a = table_a.shape
    wide_b = table_b.shape[1]
    capacity = 3 * lookups // (2 * shards)
    bags, embed = d_pooled.shape
    slots = shards * capacity
    proj = jnp.concatenate([proj_a, proj_b], axis=0)
    row_grad = dot(proj, d_pooled, ((1,), (1,))).astype(BF16)
    held_a = onehot_rows(slot_of(owner_a.reshape(1, lookups), shards, capacity), slots)
    held_b = onehot_rows(slot_of(owner_b.reshape(1, lookups), shards, capacity), slots)
    bag_a, bag_b = onehot_rows(bag_a, bags), onehot_rows(bag_b, bags)
    row_a, row_b = row_a.reshape(1, lookups), row_b.reshape(1, lookups)
    none = lambda count: jnp.zeros((count, lookups), BF16)
    sent_a = jnp.concatenate(
        [
            dot(row_grad[:wide_a], bag_a, ((1,), (0,))).astype(BF16),
            none(wide_b),
            (row_a // BASE).astype(BF16),
            (row_a % BASE).astype(BF16),
            none(128 - wide_a - wide_b - 2),
        ]
    )
    sent_b = jnp.concatenate(
        [
            none(wide_a),
            dot(row_grad[wide_a:], bag_b, ((1,), (0,))).astype(BF16),
            none(2),
            (row_b // BASE).astype(BF16),
            (row_b % BASE).astype(BF16),
            none(128 - wide_a - wide_b - 4),
        ]
    )
    sent = dot(held_a, sent_a, ((1,), (1,))) + dot(held_b, sent_b, ((1,), (1,)))
    came = exchange(sent.astype(BF16).reshape(shards, capacity, 128), "shard").reshape(slots, 128)
    wanted = came[:, wide_a + wide_b : wide_a + wide_b + 4].astype(jnp.int32)
    row_hot_a = onehot_columns(wanted[:, 0:1] * BASE + wanted[:, 1:2], rows)
    row_hot_b = onehot_columns(wanted[:, 2:3] * BASE + wanted[:, 3:4], rows)
    gathered = jnp.concatenate(
        [
            dot(row_hot_a, table_a, ((1,), (0,))).astype(BF16),
            dot(row_hot_b, table_b, ((1,), (0,))).astype(BF16),
            jnp.zeros((slots, 128 - wide_a - wide_b), BF16),
        ],
        axis=1,
    )
    back = exchange(gathered.reshape(shards, capacity, 128), "shard").reshape(slots, 128)
    grads = jnp.concatenate(
        [
            dot(came[:, :wide_a], row_hot_a, ((0,), (0,))),
            dot(came[:, wide_a : wide_a + wide_b], row_hot_b, ((0,), (0,))),
        ]
    ).astype(BF16)
    wide = wide_a + wide_b
    pieces = grads.reshape(wide, replicas, rows // replicas).transpose(1, 0, 2)
    share = jnp.sum(exchange(pieces, "rep").astype(F32), axis=0).astype(BF16)
    grads = spread(share, "rep").transpose(1, 0, 2).reshape(wide, rows).astype(F32)
    looked_a = dot(back[:, :wide_a], held_a, ((0,), (0,))).astype(BF16)
    looked_b = dot(back[:, wide_a:wide], held_b, ((0,), (0,))).astype(BF16)
    summed = jnp.concatenate([dot(looked_a, bag_a, ((1,), (1,))), dot(looked_b, bag_b, ((1,), (1,)))])
    high = summed.astype(BF16)
    low = (summed - high.astype(F32)).astype(BF16)
    pooled = dot(high, proj, ((0,), (0,))) + dot(low, proj, ((0,), (0,)))
    partial = dot(high, d_pooled, ((1,), (0,))) + dot(low, d_pooled, ((1,), (0,)))
    part = jnp.sum(exchange(partial.reshape(shards, -1), "shard"), axis=0)
    part = jnp.sum(spread(part, "rep"), axis=0)
    part = part / jnp.sqrt(F32(lookups * shards * replicas))
    grad_proj = spread(part, "shard").reshape(wide, embed)
    return (
        pooled.astype(BF16),
        grads[:wide_a].T,
        grads[wide_a:].T,
        grad_proj[:wide_a],
        grad_proj[wide_a:],
    )


def solution(mesh):
    split = ("shard", "rep")
    tier = (P(split, None), P(split), P(split, None))
    in_specs = (P("shard", None), P("shard", None), P(), P(), *tier, *tier, P(split, None))
    out_specs = (P(split, None), P("shard", None), P("shard", None), P(), P())
    return jax.shard_map(body, mesh=mesh, in_specs=in_specs, out_specs=out_specs, check_vma=False)
```

time: 807 us -> 177 us (0.22)
  the two profiles are of different devices: /device:TPU:1 before, /device:TPU:64 now
where the time goes in v1:
time: 177 us; the launch traced here: 176 us
  waiting for transfers between devices  91.4 us (52%)
  starting transfers between devices  55.4 us (31%)
  matrix products  16.2 us (9%)
  local copies, waits for them, and re-layouts  8.81 us (5%)
  other arithmetic  3.53 us (2%)
    all_to_all x7, waiting for transfers between devices, exchange(): return lax.all_to_all(x, axis, split_axis=0, concat_axis=0, tiled=True)  91.4 us
    all_to_all x7, starting transfers between devices, exchange(): return lax.all_to_all(x, axis, split_axis=0, concat_axis=0, tiled=True)  55.4 us
    dot_general x17, matrix products, dot(): lax.dot_general(left, right, (dims, ((), ())), preferred_element_type=F32)  16.2 us
  transfers between devices with their start and end apart: 7, of which 7 were waited for; matrix products, arithmetic and copies ran while one was open for 4% of the time, Pallas kernels for 0%

profile of v1, /device:TPU:64, one launch (start us, length us, event | category | flops | bytes accessed | tf_op | source)
XLA Modules:
  0.0 176.4 jit_solution(2247011641543617379)
XLA Ops:
  2.2 1.2 fusion.32
  5.5 1.1 fusion.5
  6.9 2.0 %fusion.19 = bf16[1536,128]{1,0:T(8,128)(2,1)} fusion(f32[1536,128]{1,0:T(8,128)S(1)} %fusion.5, bf16[128,1024]{1,0:T(8,128)(2,1)S(1)} %concatenate.25, s32[1024]{0:T(1024)S(1)} %convert_add_fusion.1), kind=kOutput, calls=%fused_computation.24 | convolution fusion | flops 404619264 | bytes 1445888 | tf_op jit(solution)/shard_map/dot_general | solution.py:11
  8.9 10.6 %all-to-all-start = ((bf16[64,24,128]{2,1,0:T(8,128)(2,1)}), bf16[64,24,128]{2,1,0:T(8,128)(2,1)S(1)}, u32[]{:S(2)}, u32[]{:S(2)}) async-start(bf16[64,24,128]{2,1,0:T(8,128)(2,1)} %bitcast.4), calls=%async_computation | async-start | bytes 786432 | tf_op jit(solution)/shard_map/all_to_all | solution.py:36
  19.5 14.8 %all-to-all-done = bf16[64,24,128]{2,1,0:T(8,128)(2,1)S(1)} async-done(((bf16[64,24,128]{2,1,0:T(8,128)(2,1)}), bf16[64,24,128]{2,1,0:T(8,128)(2,1)S(1)}, u32[]{:S(2)}, u32[]{:S(2)}) %all-to-all-start) | async-done | bytes 393248 | tf_op jit(solution)/shard_map/all_to_all | solution.py:36
  34.5 1.1 fusion.42
  35.7 1.4 fusion.20
  37.1 1.4 fusion.21
  39.5 6.0 %all-to-all-start.1 = ((bf16[64,24,128]{2,1,0:T(8,128)(2,1)}), bf16[64,24,128]{2,1,0:T(8,128)(2,1)S(1)}, u32[]{:S(2)}, u32[]{:S(2)}) async-start(bf16[64,24,128]{2,1,0:T(8,128)(2,1)} %bitcast.6), calls=%async_computation.1 | async-start | bytes 786432 | tf_op jit(solution)/shard_map/all_to_all | solution.py:36
  45.5 1.2 fusion.30
  46.9 13.3 %all-to-all-done.1 = bf16[64,24,128]{2,1,0:T(8,128)(2,1)S(1)} async-done(((bf16[64,24,128]{2,1,0:T(8,128)(2,1)}), bf16[64,24,128]{2,1,0:T(8,128)(2,1)S(1)}, u32[]{:S(2)}, u32[]{:S(2)}) %all-to-all-start.1) | async-done | bytes 393248 | tf_op jit(solution)/shard_map/all_to_all | solution.py:36
  60.2 1.6 fusion.24
  61.8 1.7 fusion.22
  64.7 5.8 %all-to-all-start.4 = ((f32[64,1,384]{2,1,0:T(1,128)}), f32[64,1,384]{2,1,0:T(1,128)S(1)}, u32[]{:S(2)}, u32[]{:S(2)}) async-start(f32[64,1,384]{2,1,0:T(1,128)} %all_to_all.34), calls=%async_computation.4 | async-start | bytes 196608 | tf_op jit(solution)/shard_map/all_to_all | solution.py:36
  70.4 1.4 fusion.36
  72.1 8.9 %all-to-all-done.4 = f32[64,1,384]{2,1,0:T(1,128)S(1)} async-done(((f32[64,1,384]{2,1,0:T(1,128)}), f32[64,1,384]{2,1,0:T(1,128)S(1)}, u32[]{:S(2)}, u32[]{:S(2)}) %all-to-all-start.4) | async-done | bytes 98336 | tf_op jit(solution)/shard_map/all_to_all | solution.py:36
  81.7 18.4 %all-to-all-start.5 = ((f32[16,1,384]{2,1,0:T(1,128)}), f32[16,1,384]{2,1,0:T(1,128)S(1)}, u32[]{:S(2)}, u32[]{:S(2)}) async-start(f32[16,1,384]{2,1,0:T(1,128)} %broadcast_in_dim.51), calls=%async_computation.5 | async-start | bytes 49152 | tf_op jit(solution)/shard_map/all_to_all | solution.py:36
  101.0 10.5 %all-to-all-done.5 = f32[16,1,384]{2,1,0:T(1,128)S(1)} async-done(((f32[16,1,384]{2,1,0:T(1,128)}), f32[16,1,384]{2,1,0:T(1,128)S(1)}, u32[]{:S(2)}, u32[]{:S(2)}) %all-to-all-start.5) | async-done | bytes 24608 | tf_op jit(solution)/shard_map/all_to_all | solution.py:36
  111.5 4.6 %all-to-all-start.2 = ((bf16[16,96,64]{1,2,0:T(8,128)(2,1)}), bf16[16,96,64]{1,2,0:T(8,128)(2,1)S(1)}, u32[]{:S(2)}, u32[]{:S(2)}) async-start(bf16[16,96,64]{1,2,0:T(8,128)(2,1)} %maximum_bitcast_fusion), calls=%async_computation.2 | async-start | bytes 524288 | tf_op jit(solution)/shard_map/all_to_all | solution.py:36
  116.2 17.9 %all-to-all-done.2 = bf16[16,96,64]{1,2,0:T(8,128)(2,1)S(1)} async-done(((bf16[16,96,64]{1,2,0:T(8,128)(2,1)}), bf16[16,96,64]{1,2,0:T(8,128)(2,1)S(1)}, u32[]{:S(2)}, u32[]{:S(2)}) %all-to-all-start.2) | async-done | bytes 196640 | tf_op jit(solution)/shard_map/all_to_all | solution.py:36
  134.8 4.6 %all-to-all-start.6 = ((f32[64,1,384]{2,1,0:T(1,128)}), f32[64,1,384]{2,1,0:T(1,128)S(1)}, u32[]{:S(2)}, u32[]{:S(2)}) async-start(f32[64,1,384]{2,1,0:T(1,128)} %broadcast_in_dim.52), calls=%async_computation.6 | async-start | bytes 196608 | tf_op jit(solution)/shard_map/all_to_all | solution.py:36
  139.5 10.5 %all-to-all-done.6 = f32[64,1,384]{2,1,0:T(1,128)S(1)} async-done(((f32[64,1,384]{2,1,0:T(1,128)}), f32[64,1,384]{2,1,0:T(1,128)S(1)}, u32[]{:S(2)}, u32[]{:S(2)}) %all-to-all-start.6) | async-done | bytes 98336 | tf_op jit(solution)/shard_map/all_to_all | solution.py:36
  150.7 5.4 %all-to-all-start.3 = ((bf16[16,96,64]{1,2,0:T(8,128)(2,1)}), bf16[16,96,64]{1,2,0:T(8,128)(2,1)S(1)}, u32[]{:S(2)}, u32[]{:S(2)}) async-start(bf16[16,96,64]{1,2,0:T(8,128)(2,1)} %broadcast_in_dim.50), calls=%async_computation.3 | async-start | bytes 524288 | tf_op jit(solution)/shard_map/all_to_all | solution.py:36
  158.8 15.6 %all-to-all-done.3 = bf16[16,96,64]{1,2,0:T(8,128)(2,1)S(1)} async-done(((bf16[16,96,64]{1,2,0:T(8,128)(2,1)}), bf16[16,96,64]{1,2,0:T(8,128)(2,1)S(1)}, u32[]{:S(2)}, u32[]{:S(2)}) %all-to-all-start.3) | async-done | bytes 196640 | tf_op jit(solution)/shard_map/all_to_all | solution.py:36
  (67 shorter events, 14.3 us)
Async XLA Ops:
  0.6 2.8 %copy-start = (bf16[512,256]{1,0:T(8,128)(2,1)S(1)}, bf16[512,256]{1,0:T(8,128)(2,1)}, u32[]{:S(2)}) copy-start(bf16[512,256]{1,0:T(8,128)(2,1)} %param.21) | copy-start | bytes 786436
  2.2 1.2 copy-start.2
  2.2 1.2 copy-start.1
  2.2 1.5 copy-start.8
  3.4 0.8 copy-start.7
  3.7 1.0 copy-start.4
  3.7 1.1 copy-start.3
  8.9 25.4 %all-to-all-start = ((bf16[64,24,128]{2,1,0:T(8,128)(2,1)}), bf16[64,24,128]{2,1,0:T(8,128)(2,1)S(1)}, u32[]{:S(2)}, u32[]{:S(2)}) async-start(bf16[64,24,128]{2,1,0:T(8,128)(2,1)} %bitcast.4), calls=%async_computation | async-start | bytes 786432 | tf_op jit(solution)/shard_map/all_to_all | solution.py:36
  34.5 1.2 copy-start.5
  35.7 1.4 copy-start.6
  39.5 20.7 %all-to-all-start.1 = ((bf16[64,24,128]{2,1,0:T(8,128)(2,1)}), bf16[64,24,128]{2,1,0:T(8,128)(2,1)S(1)}, u32[]{:S(2)}, u32[]{:S(2)}) async-start(bf16[64,24,128]{2,1,0:T(8,128)(2,1)} %bitcast.6), calls=%async_computation.1 | async-start | bytes 786432 | tf_op jit(solution)/shard_map/all_to_all | solution.py:36
  64.7 16.3 %all-to-all-start.4 = ((f32[64,1,384]{2,1,0:T(1,128)}), f32[64,1,384]{2,1,0:T(1,128)S(1)}, u32[]{:S(2)}, u32[]{:S(2)}) async-start(f32[64,1,384]{2,1,0:T(1,128)} %all_to_all.34), calls=%async_computation.4 | async-start | bytes 196608 | tf_op jit(solution)/shard_map/all_to_all | solution.py:36
  81.7 29.8 %all-to-all-start.5 = ((f32[16,1,384]{2,1,0:T(1,128)}), f32[16,1,384]{2,1,0:T(1,128)S(1)}, u32[]{:S(2)}, u32[]{:S(2)}) async-start(f32[16,1,384]{2,1,0:T(1,128)} %broadcast_in_dim.51), calls=%async_computation.5 | async-start | bytes 49152 | tf_op jit(solution)/shard_map/all_to_all | solution.py:36
  111.5 22.6 %all-to-all-start.2 = ((bf16[16,96,64]{1,2,0:T(8,128)(2,1)}), bf16[16,96,64]{1,2,0:T(8,128)(2,1)S(1)}, u32[]{:S(2)}, u32[]{:S(2)}) async-start(bf16[16,96,64]{1,2,0:T(8,128)(2,1)} %maximum_bitcast_fusion), calls=%async_computation.2 | async-start | bytes 524288 | tf_op jit(solution)/shard_map/all_to_all | solution.py:36
  134.8 15.2 %all-to-all-start.6 = ((f32[64,1,384]{2,1,0:T(1,128)}), f32[64,1,384]{2,1,0:T(1,128)S(1)}, u32[]{:S(2)}, u32[]{:S(2)}) async-start(f32[64,1,384]{2,1,0:T(1,128)} %broadcast_in_dim.52), calls=%async_computation.6 | async-start | bytes 196608 | tf_op jit(solution)/shard_map/all_to_all | solution.py:36
  150.7 23.7 %all-to-all-start.3 = ((bf16[16,96,64]{1,2,0:T(8,128)(2,1)}), bf16[16,96,64]{1,2,0:T(8,128)(2,1)S(1)}, u32[]{:S(2)}, u32[]{:S(2)}) async-start(bf16[16,96,64]{1,2,0:T(8,128)(2,1)} %broadcast_in_dim.50), calls=%async_computation.3 | async-start | bytes 524288 | tf_op jit(solution)/shard_map/all_to_all | solution.py:36

commit v2 on v0

v2 whole, which is shorter than its diff:
```python
import functools

import jax
import jax.numpy as jnp
from jax import lax
from jax.experimental import pallas as pl
from jax.experimental.pallas import tpu as pltpu
from jax.sharding import PartitionSpec as P

F32, BF16, I32 = jnp.float32, jnp.bfloat16, jnp.int32
LANES = 128
SLOT_ROWS = 32
GROUPS = 8
DIGIT = 5


def dot(left, right, dims=((1,), (0,))):
    return lax.dot_general(left, right, (dims, ((), ())), preferred_element_type=F32)


def iota(shape, dim):
    return lax.broadcasted_iota(I32, shape, dim)


def onehot(hit):
    return jnp.where(hit, 1.0, 0.0).astype(BF16)


def wait_bytes(ref, sem):
    pltpu.make_async_copy(ref, ref, sem).wait()


def digits(row, first, shape):
    at = iota(shape, 0)
    high, low = lax.shift_right_logical(row, DIGIT), jnp.bitwise_and(row, (1 << DIGIT) - 1)
    return jnp.where(at == first, high, jnp.where(at == first + 1, low, 0))


def column(block, lane):
    at = iota((1, LANES), 1)
    weight = jnp.where(at == lane, float(1 << DIGIT), jnp.where(at == lane + 1, 1.0, 0.0))
    return jnp.sum(block * weight, axis=1, keepdims=True).astype(I32)


def order(step, start):
    odd = step % 2
    return (start + 4 + (1 - odd) * (step // 2) - odd * ((step + 1) // 2) + GROUPS) % GROUPS


def kernel(
    shards,
    replicas,
    tab_a, tab_b, proj_a, proj_b, owner_a, row_a, bag_a, owner_b, row_b, bag_b, d_pooled,
    pooled_out, grads_out, proj_out,
    tabs, proj, slot, give, sent, came, found, back, bags_a, bags_b, grads, looked,
    piece, piece_in, share, share_in, part, part_in, tile, tile_in, done, done_in,
    local_sem, send_sems, came_sems, back_sems, recv_sems,
):
    me, rep = lax.axis_index("shard"), lax.axis_index("rep")
    lookups, rows, bags = owner_a.shape[1], tab_a.shape[1], d_pooled.shape[0]
    wide_a, wide_b = tab_a.shape[0], tab_b.shape[0]
    wide = wide_a + wide_b
    per_group = shards // GROUPS
    slots = per_group * SLOT_ROWS
    my_group = me // per_group
    holders, per = part.shape[0], part.shape[1] // 8
    stride = shards // holders

    barrier = pltpu.get_barrier_semaphore()

    def greet_shard(step, carry):
        pl.semaphore_signal(barrier, inc=1, device_id=((me + step) % shards, rep), device_id_type=pl.DeviceIdType.MESH)
        return carry

    def greet_rep(step, carry):
        pl.semaphore_signal(barrier, inc=1, device_id=(me, (rep + step) % replicas), device_id_type=pl.DeviceIdType.MESH)
        return carry

    lax.fori_loop(1, shards, greet_shard, 0)
    lax.fori_loop(1, replicas, greet_rep, 0)

    proj[0:wide_a, :] = proj_a[...]
    proj[wide_a:wide, :] = proj_b[...]
    proj[wide:, :] = jnp.zeros((LANES - wide, proj.shape[1]), BF16)
    tabs[...] = jnp.zeros_like(tabs)
    tabs[0, 0:wide_a, :] = tab_a[...]
    tabs[1, wide_a:wide, :] = tab_b[...]
    give[...] = jnp.zeros_like(give)

    row_grad = dot(proj[...], d_pooled[...], ((1,), (1,))).astype(BF16)
    chunk = min(256, lookups)
    before = onehot(iota((chunk, chunk), 0) < iota((chunk, chunk), 1))
    carried = jnp.zeros((2 * shards, 1), F32)
    for first in range(0, lookups, chunk):
        cut = slice(first, first + chunk)
        named_a = owner_a[:, cut] == iota((shards, chunk), 0)
        named_b = owner_b[:, cut] == iota((shards, chunk), 0)
        named = jnp.concatenate([jnp.where(named_a, 1.0, 0.0), jnp.where(named_b, 1.0, 0.0)])
        earlier = dot(named.astype(BF16), before) + carried
        carried = carried + jnp.sum(named, axis=1, keepdims=True)
        earlier = earlier * named
        place_a = jnp.sum(earlier[:shards], axis=0, keepdims=True).astype(I32)
        place_b = jnp.sum(earlier[shards:], axis=0, keepdims=True).astype(I32)
        slot[0:1, cut] = owner_a[:, cut] * SLOT_ROWS + place_a
        slot[1:2, cut] = owner_b[:, cut] * SLOT_ROWS + place_b
        in_bag = onehot(bag_a[:, cut] == iota((bags, chunk), 0))
        give[0, 0:wide_a, cut] = dot(row_grad[0:wide_a], in_bag).astype(BF16)
        in_bag = onehot(bag_b[:, cut] == iota((bags, chunk), 0))
        give[1, wide_a:wide, cut] = dot(row_grad[wide_a:wide], in_bag).astype(BF16)
        tail = (LANES - wide, chunk)
        give[0, wide:, cut] = (digits(row_a[:, cut], 0, tail) + digits(bag_a[:, cut] + 1, 2, tail)).astype(F32).astype(BF16)
        give[1, wide:, cut] = (digits(row_b[:, cut], 4, tail) + digits(bag_b[:, cut] + 1, 6, tail)).astype(F32).astype(BF16)

    pl.semaphore_wait(barrier, shards + replicas - 2)

    def to_shard(block, there, target, send_sem, recv_sem):
        pltpu.make_async_remote_copy(
            src_ref=block,
            dst_ref=there,
            send_sem=send_sem,
            recv_sem=recv_sem,
            device_id=(target, rep),
            device_id_type=pl.DeviceIdType.MESH,
        ).start()

    def to_rep(block, there, target, send_sem, recv_sem):
        pltpu.make_async_remote_copy(
            src_ref=block,
            dst_ref=there,
            send_sem=send_sem,
            recv_sem=recv_sem,
            device_id=(me, target),
            device_id_type=pl.DeviceIdType.MESH,
        ).start()

    def send_group(group, source, landing, send_sem, recv_sem):
        def one(i, carry):
            target = group * per_group + i

            @pl.when(target != me)
            def _():
                to_shard(source.at[target], landing.at[me], target, send_sem, recv_sem)

            @pl.when(target == me)
            def _():
                pltpu.make_async_copy(source.at[target], landing.at[me], recv_sem).start()

            return carry

        lax.fori_loop(0, per_group, one, 0)

    def ask(step, carry):
        group = order(step, my_group)
        at = iota((slots, lookups), 0) + group * slots
        block = dot(onehot(slot[0:1, :] == at), give[0], ((1,), (1,)))
        block += dot(onehot(slot[1:2, :] == at), give[1], ((1,), (1,)))
        sent[pl.ds(group * per_group, per_group)] = block.reshape(per_group, SLOT_ROWS, LANES).astype(BF16)
        send_group(group, sent, came, send_sems.at[0], came_sems.at[my_group])
        return carry

    lax.fori_loop(0, GROUPS, ask, 0)

    grads[...] = jnp.zeros_like(grads)
    looked[...] = jnp.zeros_like(looked)

    def mark(group, carry):
        block = sent[pl.ds(group * per_group, per_group)].reshape(slots, LANES).astype(F32)
        at = iota((slots, bags), 1) + 1
        bags_a[pl.ds(group * slots, slots), :] = onehot(column(block, wide + 2) == at)
        bags_b[pl.ds(group * slots, slots), :] = onehot(column(block, wide + 6) == at)
        return carry

    lax.fori_loop(0, GROUPS, mark, 0)

    def answer(step, carry):
        group = order(step, my_group)
        mine = pl.ds(group * per_group, per_group)
        wait_bytes(came.at[mine], came_sems.at[group])
        block = came[mine].reshape(slots, LANES).astype(F32)
        at = iota((slots, rows), 1)
        hot_a = onehot(column(block, wide) == at)
        hot_b = onehot(column(block, wide + 4) == at)
        gathered = dot(hot_a, tabs[0], ((1,), (1,))) + dot(hot_b, tabs[1], ((1,), (1,)))
        found[mine] = gathered.reshape(per_group, SLOT_ROWS, LANES).astype(BF16)
        send_group(group, found, back, send_sems.at[1], back_sems.at[my_group])
        turned = block.T.astype(BF16)
        grads[0:wide_a, :] += dot(turned[0:wide_a], hot_a)
        grads[wide_a:wide, :] += dot(turned[wide_a:wide], hot_b)
        return carry

    lax.fori_loop(0, GROUPS, answer, 0)

    tall, broad = piece.shape[1], piece.shape[2]
    across = rows // broad
    for k in range(replicas):
        high, left = (k // across) * tall, (k % across) * broad
        piece[k] = grads[high : high + tall, left : left + broad].astype(BF16)
    piece_in[rep] = piece[rep]

    def scatter(step, carry):
        target = (rep + step) % replicas
        to_rep(piece.at[target], piece_in.at[rep], target, send_sems.at[2], recv_sems.at[0])
        return carry

    lax.fori_loop(1, replicas, scatter, 0)

    def pool(step, carry):
        group = order(step, my_group)
        mine = pl.ds(group * per_group, per_group)
        wait_bytes(back.at[mine], back_sems.at[group])
        turned = back[mine].reshape(slots, LANES).astype(F32).T.astype(BF16)
        here = pl.ds(group * slots, slots)
        looked[0:wide_a, :] += dot(turned[0:wide_a], bags_a[here, :])
        looked[wide_a:wide, :] += dot(turned[wide_a:wide], bags_b[here, :])
        return carry

    lax.fori_loop(0, GROUPS, pool, 0)

    high = looked[...].astype(BF16)
    low = (looked[...] - high.astype(F32)).astype(BF16)
    partial = dot(high, d_pooled[...]) + dot(low, d_pooled[...])
    embed = partial.shape[1]
    halves = embed // LANES
    for k in range(holders * per):
        top, left = (k // halves) * 8, (k % halves) * LANES
        part[k // per, (k % per) * 8 : (k % per) * 8 + 8, :] = partial[top : top + 8, left : left + LANES]
    index = me // stride
    holding = jnp.logical_and(me == index * stride, index < holders)

    def hand(step, carry):
        target = (index + step) % holders

        @pl.when(target * stride != me)
        def _():
            to_shard(part.at[target], part_in.at[me], target * stride, send_sems.at[4], recv_sems.at[2])

        return carry

    lax.fori_loop(0, holders, hand, 0)

    wait_bytes(piece_in.at[pl.ds(0, replicas - 1)], recv_sems.at[0])
    share[...] = jnp.sum(piece_in[...].astype(F32), axis=0).astype(BF16)
    share_in[rep] = share[...]

    def give_share(step, carry):
        to_rep(share, share_in.at[rep], (rep + step) % replicas, send_sems.at[3], recv_sems.at[1])
        return carry

    lax.fori_loop(1, replicas, give_share, 0)

    @pl.when(holding)
    def _():
        part_in[me] = part[index]
        wait_bytes(part_in.at[pl.ds(0, shards - 1)], recv_sems.at[2])
        tile[...] = jnp.sum(part_in[...], axis=0)
        tile_in[rep] = tile[...]

        def swap(step, carry):
            to_rep(tile, tile_in.at[rep], (rep + step) % replicas, send_sems.at[5], recv_sems.at[3])
            return carry

        lax.fori_loop(1, replicas, swap, 0)

    turned = looked[...].T
    high = turned.astype(BF16)
    low = (turned - high.astype(F32)).astype(BF16)
    pooled_out[...] = (dot(high, proj[...]) + dot(low, proj[...])).astype(BF16)

    @pl.when(holding)
    def _():
        wait_bytes(tile_in.at[pl.ds(0, replicas - 1)], recv_sems.at[3])
        scale = 1.0 / (float(lookups * shards * replicas) ** 0.5)
        done[...] = jnp.sum(tile_in[...], axis=0) * scale
        done_in[index] = done[...]

        def tell(step, carry):
            to_shard(done, done_in.at[index], (me + step) % shards, send_sems.at[6], recv_sems.at[4])
            return carry

        lax.fori_loop(1, shards, tell, 0)

    wait_bytes(share_in.at[pl.ds(0, replicas - 1)], recv_sems.at[1])
    for k in range(replicas):
        top, left = (k // across) * tall, (k % across) * broad
        grads_out[top : top + tall, left : left + broad] = share_in[k]

    @pl.when(holding)
    def _():
        wait_bytes(done_in.at[pl.ds(0, holders - 1)], recv_sems.at[4])

    @pl.when(jnp.logical_not(holding))
    def _():
        wait_bytes(done_in, recv_sems.at[4])

    for k in range(holders * per):
        top, left = (k // halves) * 8, (k % halves) * LANES
        proj_out[top : top + 8, left : left + LANES] = done_in[k // per, (k % per) * 8 : (k % per) * 8 + 8, :]

    wait_bytes(sent.at[pl.ds(0, shards - 1)], send_sems.at[0])
    wait_bytes(found.at[pl.ds(0, shards - 1)], send_sems.at[1])
    wait_bytes(piece.at[pl.ds(0, replicas - 1)], send_sems.at[2])
    wait_bytes(share_in.at[pl.ds(0, replicas - 1)], send_sems.at[3])

    @pl.when(holding)
    def _():
        wait_bytes(part.at[pl.ds(0, holders - 1)], send_sems.at[4])
        wait_bytes(tile_in.at[pl.ds(0, replicas - 1)], send_sems.at[5])
        wait_bytes(part_in.at[pl.ds(0, shards - 1)], send_sems.at[6])

    @pl.when(jnp.logical_not(holding))
    def _():
        wait_bytes(part, send_sems.at[4])


def body(table_a, table_b, proj_a, proj_b, owner_a, row_a, bag_a, owner_b, row_b, bag_b, d_pooled):
    shards, replicas = lax.axis_size("shard"), lax.axis_size("rep")
    lookups = row_a.shape[0]
    rows, wide_a = table_a.shape
    wide = wide_a + table_b.shape[1]
    bags, embed = d_pooled.shape
    tiles = wide * embed // (8 * LANES)
    holders = min(tiles, shards)
    per = tiles // holders
    tall, broad = wide // 2, 2 * rows // replicas
    block = pltpu.VMEM((shards, SLOT_ROWS, LANES), BF16)
    line = (1, lookups)
    pooled, grads, grad_proj = pl.pallas_call(
        functools.partial(kernel, shards, replicas),
        out_shape=(
            jax.ShapeDtypeStruct((bags, embed), BF16),
            jax.ShapeDtypeStruct((wide, rows), BF16),
            jax.ShapeDtypeStruct((wide, embed), F32),
        ),
        in_specs=[pl.BlockSpec(memory_space=pltpu.VMEM)] * 11,
        out_specs=(pl.BlockSpec(memory_space=pltpu.VMEM),) * 3,
        scratch_shapes=[
            pltpu.VMEM((2, LANES, rows), BF16),
            pltpu.VMEM((LANES, embed), BF16),
            pltpu.VMEM((8, lookups), I32),
            pltpu.VMEM((2, LANES, lookups), BF16),
            block,
            block,
            block,
            block,
            pltpu.VMEM((shards * SLOT_ROWS, bags), BF16),
            pltpu.VMEM((shards * SLOT_ROWS, bags), BF16),
            pltpu.VMEM((wide, rows), F32),
            pltpu.VMEM((LANES, bags), F32),
            pltpu.VMEM((replicas, tall, broad), BF16),
            pltpu.VMEM((replicas, tall, broad), BF16),
            pltpu.VMEM((tall, broad), BF16),
            pltpu.VMEM((replicas, tall, broad), BF16),
            pltpu.VMEM((holders, 8 * per, LANES), F32),
            pltpu.VMEM((shards, 8 * per, LANES), F32),
            pltpu.VMEM((8 * per, LANES), F32),
            pltpu.VMEM((replicas, 8 * per, LANES), F32),
            pltpu.VMEM((8 * per, LANES), F32),
            pltpu.VMEM((holders, 8 * per, LANES), F32),
            pltpu.SemaphoreType.DMA((1,)),
            pltpu.SemaphoreType.DMA((7,)),
            pltpu.SemaphoreType.DMA((GROUPS,)),
            pltpu.SemaphoreType.DMA((GROUPS,)),
            pltpu.SemaphoreType.DMA((5,)),
        ],
        compiler_params=pltpu.CompilerParams(
            collective_id=0, has_side_effects=True, vmem_limit_bytes=48 * 1024 * 1024
        ),
    )(
        table_a.T,
        table_b.T,
        proj_a,
        proj_b,
        owner_a.reshape(line),
        row_a.reshape(line),
        bag_a,
        owner_b.reshape(line),
        row_b.reshape(line),
        bag_b,
        d_pooled,
    )
    grads = grads.astype(F32).T
    return (pooled, grads[:, :wide_a], grads[:, wide_a:], grad_proj[:wide_a], grad_proj[wide_a:])


def solution(mesh):
    split = ("shard", "rep")
    tier = (P(split, None), P(split), P(split, None))
    in_specs = (P("shard", None), P("shard", None), P(), P(), *tier, *tier, P(split, None))
    out_specs = (P(split, None), P("shard", None), P("shard", None), P(), P())
    return jax.shard_map(body, mesh=mesh, in_specs=in_specs, out_specs=out_specs, check_vma=False)
```

time: 807 us -> 92.9 us (0.12); the launches traced: 797 us -> 92.4 us
  waiting for transfers between devices: 487 us -> 0 us
  blocking collectives: 131 us -> 0 us
  Pallas kernels: 0 us -> 80.8 us
  other arithmetic: 58.8 us -> 0.03 us
  starting transfers between devices: 51.2 us -> 0 us
  local copies, waits for them, and re-layouts: 45.2 us -> 10.9 us
  between operations: 14.5 us -> 0.68 us
  matrix products: 9.19 us -> 0 us
    psum x2 -> x0, waiting for transfers between devices: 428 us -> none  [the longest x1 301 us: body(): summed_a, summed_b = lax.psum((partial_a, partial_b), ('shard', 'rep'))]
    psum x1 -> x0, blocking collectives: 131 us -> none  [body(): summed_a, summed_b = lax.psum((partial_a, partial_b), ('shard', 'rep'))]
    pallas_call x0 -> x1, Pallas kernels: none -> 80.8 us  [body(): pl.pallas_call(functools.partial(kernel, shards, replicas), out_shape=(ja...]
    all_to_all x6 -> x0, waiting for transfers between devices: 58.9 us -> none  [the longest x1 18 us: body(): lax.all_to_all(lift_rows(fetched_b, proj_b), 'shard', split_axis=0, conca...]
    all_to_all x6 -> x0, starting transfers between devices: 51.1 us -> none  [the longest x1 18.2 us: body(): lax.all_to_all(request_b, 'shard', split_axis=0, concat_axis=0, tiled=True)]
    another operation x6 -> x0, other arithmetic: 36.4 us -> none
    scatter-add x2 -> x0, other arithmetic: 19.2 us -> none  [the longest x1 9.58 us: body(): jnp.zeros(table_b.shape, jnp.float32).at[wanted_b]]
    gather x4 -> x0, local copies, waits for them, and re-layouts: 18 us -> none  [the longest x1 5.82 us: body(): lifted_a = slots_a[owners_a, position_a]]
  transfers between devices with their start and end apart: 8 -> 0, of which waited for: 7 -> 0; matrix products, arithmetic and copies ran while one was open for 8% -> 0% of each run, Pallas kernels for 0% -> 0%
where the time goes in v2:
time: 92.9 us; the launch traced here: 92.4 us
  Pallas kernels  80.8 us (87%)
  local copies, waits for them, and re-layouts  10.9 us (12%)
    pallas_call x1, Pallas kernels, body(): pl.pallas_call(functools.partial(kernel, shards, replicas), out_shape=(ja...  80.8 us
    unnamed x23, local copies, waits for them, and re-layouts  8.3 us

profile of v2, /device:TPU:1, one launch (start us, length us, event | category | flops | bytes accessed | tf_op | source)
XLA Modules:
  0.0 92.4 jit_solution(13952271948714288018)
XLA Ops:
  0.6 0.0 copy-start.6
  0.6 0.0 copy-start.5
  0.7 0.7 copy-done.6
  1.3 0.0 copy-done.5
  1.3 0.0 copy-start
  1.3 0.9 %copy-done = bf16[512,256]{1,0:T(8,128)(2,1)S(1)} copy-done((bf16[512,256]{1,0:T(8,128)(2,1)S(1)}, bf16[512,256]{1,0:T(8,128)(2,1)}, u32[]{:S(2)}) %copy-start) | copy-done | bytes 262168
  2.3 0.0 copy-start.1
  2.3 0.9 copy-done.1
  3.2 0.0 copy-start.2
  3.2 0.8 copy-done.2
  4.0 0.0 copy-start.3
  4.0 0.8 copy-done.3
  4.8 0.0 copy-start.4
  4.8 0.7 copy-done.4
  5.5 0.7 copy-done.7
  6.2 0.7 copy-done.8
  6.9 0.7 copy-done.9
  7.6 0.7 copy-done.10
  8.3 80.8 %shard_map.146 = (bf16[512,256]{1,0:T(8,128)(2,1)S(1)}, bf16[96,1024]{1,0:T(8,128)(2,1)S(1)}, f32[96,256]{1,0:T(8,128)S(1)}) custom-call(bf16[64,1024]{1,0:T(8,128)(2,1)S(1)} %bitcast.8, bf16[32,1024]{1,0:T(8,128)(2,1)S(1)} %bitcast.9, bf16[64,256]{1,0:T(8,128)(2,1)S(1)} %copy-done.3, bf16[32,256]{1,0:T(8,128)(2,1)S(1)} %copy-done.4, ...), custom_call_target="tpu_custom_call" | custom-call | tf_op jit(solution)/shard_map/pallas_call | solution.py:327
  89.0 0.6 slice.15
  89.6 0.6 slice.14
  90.3 0.7 slice.17
  91.0 0.7 slice.16
  91.7 0.7 copy.17
  (5 shorter events, 0.0 us)
Async XLA Ops:
  0.6 0.7 copy-start.6
  0.6 0.7 copy-start.5
  1.3 0.9 %copy-start = (bf16[512,256]{1,0:T(8,128)(2,1)S(1)}, bf16[512,256]{1,0:T(8,128)(2,1)}, u32[]{:S(2)}) copy-start(bf16[512,256]{1,0:T(8,128)(2,1)} %d_pooled.1) | copy-start | bytes 786436
  2.3 0.9 copy-start.1
  3.2 0.8 copy-start.2
  4.0 0.8 copy-start.3
  4.8 0.7 copy-start.4
  5.5 0.7 copy-start.7
  6.2 0.7 copy-start.8
  6.9 0.7 copy-start.9
  7.6 0.7 copy-start.10

commit v3 on v2

--- a/solution.py
+++ b/solution.py
@@ -9,9 +9,10 @@
 
 F32, BF16, I32 = jnp.float32, jnp.bfloat16, jnp.int32
 LANES = 128
-SLOT_ROWS = 32
+SLOT_ROWS = 24
 GROUPS = 8
 DIGIT = 5
+VMEM = 64 * 1024 * 1024
 
 
 def dot(left, right, dims=((1,), (0,))):
@@ -50,11 +51,12 @@
 def kernel(
     shards,
     replicas,
-    tab_a, tab_b, proj_a, proj_b, owner_a, row_a, bag_a, owner_b, row_b, bag_b, d_pooled,
+    tab_a, tab_b, proj_a, proj_b, owner_a_in, row_a_in, bag_a_in, owner_b_in, row_b_in, bag_b_in, d_pooled_in,
     pooled_out, grads_out, proj_out,
+    owner_a, row_a, bag_a, owner_b, row_b, bag_b, d_pooled,
     tabs, proj, slot, give, sent, came, found, back, bags_a, bags_b, grads, looked,
     piece, piece_in, share, share_in, part, part_in, tile, tile_in, done, done_in,
-    local_sem, send_sems, came_sems, back_sems, recv_sems,
+    in_sems, send_sems, came_sems, back_sems, recv_sems,
 ):
     me, rep = lax.axis_index("shard"), lax.axis_index("rep")
     lookups, rows, bags = owner_a.shape[1], tab_a.shape[1], d_pooled.shape[0]
@@ -66,6 +68,26 @@
     holders, per = part.shape[0], part.shape[1] // 8
     stride = shards // holders
 
+    loads = [
+        pltpu.make_async_copy(source, target, in_sems.at[k])
+        for k, (source, target) in enumerate(
+            (
+                (owner_a_in, owner_a),
+                (owner_b_in, owner_b),
+                (bag_a_in, bag_a),
+                (bag_b_in, bag_b),
+                (row_a_in, row_a),
+                (row_b_in, row_b),
+                (proj_a, proj.at[0:wide_a]),
+                (proj_b, proj.at[wide_a:wide]),
+                (d_pooled_in, d_pooled),
+                (tab_a, tabs.at[0, 0:wide_a]),
+                (tab_b, tabs.at[1, wide_a:wide]),
+            )
+        )
+    ]
+    for load in loads:
+        load.start()
     barrier = pltpu.get_barrier_semaphore()
 
     def greet_shard(step, carry):
@@ -79,13 +101,14 @@
     lax.fori_loop(1, shards, greet_shard, 0)
     lax.fori_loop(1, replicas, greet_rep, 0)
 
-    proj[0:wide_a, :] = proj_a[...]
-    proj[wide_a:wide, :] = proj_b[...]
     proj[wide:, :] = jnp.zeros((LANES - wide, proj.shape[1]), BF16)
-    tabs[...] = jnp.zeros_like(tabs)
-    tabs[0, 0:wide_a, :] = tab_a[...]
-    tabs[1, wide_a:wide, :] = tab_b[...]
-    give[...] = jnp.zeros_like(give)
+    tabs[0, wide_a:, :] = jnp.zeros((LANES - wide_a, rows), BF16)
+    tabs[1, 0:wide_a, :] = jnp.zeros((wide_a, rows), BF16)
+    tabs[1, wide:, :] = jnp.zeros((LANES - wide, rows), BF16)
+    give[0, wide_a:wide, :] = jnp.zeros((wide - wide_a, lookups), BF16)
+    give[1, 0:wide_a, :] = jnp.zeros((wide_a, lookups), BF16)
+    for load in loads[:9]:
+        load.wait()
 
     row_grad = dot(proj[...], d_pooled[...], ((1,), (1,))).astype(BF16)
     chunk = min(256, lookups)
@@ -163,20 +186,14 @@
     grads[...] = jnp.zeros_like(grads)
     looked[...] = jnp.zeros_like(looked)
 
-    def mark(group, carry):
-        block = sent[pl.ds(group * per_group, per_group)].reshape(slots, LANES).astype(F32)
-        at = iota((slots, bags), 1) + 1
-        bags_a[pl.ds(group * slots, slots), :] = onehot(column(block, wide + 2) == at)
-        bags_b[pl.ds(group * slots, slots), :] = onehot(column(block, wide + 6) == at)
-        return carry
-
-    lax.fori_loop(0, GROUPS, mark, 0)
+    for load in loads[9:]:
+        load.wait()
 
     def answer(step, carry):
         group = order(step, my_group)
         mine = pl.ds(group * per_group, per_group)
         wait_bytes(came.at[mine], came_sems.at[group])
-        block = came[mine].reshape(slots, LANES).astype(F32)
+        block = came[mine].astype(F32).reshape(slots, LANES)
         at = iota((slots, rows), 1)
         hot_a = onehot(column(block, wide) == at)
         hot_b = onehot(column(block, wide + 4) == at)
@@ -204,11 +221,20 @@
 
     lax.fori_loop(1, replicas, scatter, 0)
 
+    def mark(group, carry):
+        block = sent[pl.ds(group * per_group, per_group)].astype(F32).reshape(slots, LANES)
+        at = iota((slots, bags), 1) + 1
+        bags_a[pl.ds(group * slots, slots), :] = onehot(column(block, wide + 2) == at)
+        bags_b[pl.ds(group * slots, slots), :] = onehot(column(block, wide + 6) == at)
+        return carry
+
+    lax.fori_loop(0, GROUPS, mark, 0)
+
     def pool(step, carry):
         group = order(step, my_group)
         mine = pl.ds(group * per_group, per_group)
         wait_bytes(back.at[mine], back_sems.at[group])
-        turned = back[mine].reshape(slots, LANES).astype(F32).T.astype(BF16)
+        turned = back[mine].astype(F32).reshape(slots, LANES).T.astype(BF16)
         here = pl.ds(group * slots, slots)
         looked[0:wide_a, :] += dot(turned[0:wide_a], bags_a[here, :])
         looked[wide_a:wide, :] += dot(turned[wide_a:wide], bags_b[here, :])
@@ -238,16 +264,6 @@
 
     lax.fori_loop(0, holders, hand, 0)
 
-    wait_bytes(piece_in.at[pl.ds(0, replicas - 1)], recv_sems.at[0])
-    share[...] = jnp.sum(piece_in[...].astype(F32), axis=0).astype(BF16)
-    share_in[rep] = share[...]
-
-    def give_share(step, carry):
-        to_rep(share, share_in.at[rep], (rep + step) % replicas, send_sems.at[3], recv_sems.at[1])
-        return carry
-
-    lax.fori_loop(1, replicas, give_share, 0)
-
     @pl.when(holding)
     def _():
         part_in[me] = part[index]
@@ -261,24 +277,34 @@
 
         lax.fori_loop(1, replicas, swap, 0)
 
+    wait_bytes(piece_in.at[pl.ds(0, replicas - 1)], recv_sems.at[0])
+    share[...] = jnp.sum(piece_in[...].astype(F32), axis=0).astype(BF16)
+    share_in[rep] = share[...]
+
+    def give_share(step, carry):
+        to_rep(share, share_in.at[rep], (rep + step) % replicas, send_sems.at[3], recv_sems.at[1])
+        return carry
+
+    lax.fori_loop(1, replicas, give_share, 0)
+
+    @pl.when(holding)
+    def _():
+        wait_bytes(tile_in.at[pl.ds(0, replicas - 1)], recv_sems.at[3])
+        scale = 1.0 / (float(lookups * shards * replicas) ** 0.5)
+        done[...] = jnp.sum(tile_in[...], axis=0) * scale
+        done_in[index] = done[...]
+
+        def tell(step, carry):
+            to_shard(done, done_in.at[index], (me + step) % shards, send_sems.at[6], recv_sems.at[4])
+            return carry
+
+        lax.fori_loop(1, shards, tell, 0)
+
     turned = looked[...].T
     high = turned.astype(BF16)
     low = (turned - high.astype(F32)).astype(BF16)
     pooled_out[...] = (dot(high, proj[...]) + dot(low, proj[...])).astype(BF16)
 
-    @pl.when(holding)
-    def _():
-        wait_bytes(tile_in.at[pl.ds(0, replicas - 1)], recv_sems.at[3])
-        scale = 1.0 / (float(lookups * shards * replicas) ** 0.5)
-        done[...] = jnp.sum(tile_in[...], axis=0) * scale
-        done_in[index] = done[...]
-
-        def tell(step, carry):
-            to_shard(done, done_in.at[index], (me + step) % shards, send_sems.at[6], recv_sems.at[4])
-            return carry
-
-        lax.fori_loop(1, shards, tell, 0)
-
     wait_bytes(share_in.at[pl.ds(0, replicas - 1)], recv_sems.at[1])
     for k in range(replicas):
         top, left = (k // across) * tall, (k % across) * broad
@@ -310,6 +336,15 @@
     @pl.when(jnp.logical_not(holding))
     def _():
         wait_bytes(part, send_sems.at[4])
+
+
+def finish(pooled, grads, grad_proj, pooled_out, grad_a, grad_b, proj_a, proj_b):
+    wide_a = grad_a.shape[0]
+    pooled_out[...] = pooled[...]
+    grad_a[...] = grads[0:wide_a, :].astype(F32)
+    grad_b[...] = grads[wide_a:, :].astype(F32)
+    proj_a[...] = grad_proj[0:wide_a, :]
+    proj_b[...] = grad_proj[wide_a:, :]
 
 
 def body(table_a, table_b, proj_a, proj_b, owner_a, row_a, bag_a, owner_b, row_b, bag_b, d_pooled):
@@ -331,9 +366,16 @@
             jax.ShapeDtypeStruct((wide, rows), BF16),
             jax.ShapeDtypeStruct((wide, embed), F32),
         ),
-        in_specs=[pl.BlockSpec(memory_space=pltpu.VMEM)] * 11,
+        in_specs=[pl.BlockSpec(memory_space=pltpu.HBM)] * 11,
         out_specs=(pl.BlockSpec(memory_space=pltpu.VMEM),) * 3,
         scratch_shapes=[
+            pltpu.VMEM(line, I32),
+            pltpu.VMEM(line, I32),
+            pltpu.VMEM(line, I32),
+            pltpu.VMEM(line, I32),
+            pltpu.VMEM(line, I32),
+            pltpu.VMEM(line, I32),
+            pltpu.VMEM((bags, embed), BF16),
             pltpu.VMEM((2, LANES, rows), BF16),
             pltpu.VMEM((LANES, embed), BF16),
             pltpu.VMEM((8, lookups), I32),
@@ -356,14 +398,14 @@
             pltpu.VMEM((replicas, 8 * per, LANES), F32),
             pltpu.VMEM((8 * per, LANES), F32),
             pltpu.VMEM((holders, 8 * per, LANES), F32),
-            pltpu.SemaphoreType.DMA((1,)),
+            pltpu.SemaphoreType.DMA((11,)),
             pltpu.SemaphoreType.DMA((7,)),
             pltpu.SemaphoreType.DMA((GROUPS,)),
             pltpu.SemaphoreType.DMA((GROUPS,)),
             pltpu.SemaphoreType.DMA((5,)),
         ],
         compiler_params=pltpu.CompilerParams(
-            collective_id=0, has_side_effects=True, vmem_limit_bytes=48 * 1024 * 1024
+            collective_id=0, has_side_effects=True, vmem_limit_bytes=VMEM
         ),
     )(
         table_a.T,
@@ -378,8 +420,20 @@
         bag_b,
         d_pooled,
     )
-    grads = grads.astype(F32).T
-    return (pooled, grads[:, :wide_a], grads[:, wide_a:], grad_proj[:wide_a], grad_proj[wide_a:])
+    pooled, grad_a, grad_b, proj_grad_a, proj_grad_b = pl.pallas_call(
+        finish,
+        out_shape=(
+            jax.ShapeDtypeStruct((bags, embed), BF16),
+            jax.ShapeDtypeStruct((wide_a, rows), F32),
+            jax.ShapeDtypeStruct((wide - wide_a, rows), F32),
+            jax.ShapeDtypeStruct((wide_a, embed), F32),
+            jax.ShapeDtypeStruct((wide - wide_a, embed), F32),
+        ),
+        in_specs=[pl.BlockSpec(memory_space=pltpu.VMEM)] * 3,
+        out_specs=(pl.BlockSpec(memory_space=pltpu.VMEM),) * 5,
+        compiler_params=pltpu.CompilerParams(vmem_limit_bytes=VMEM),
+    )(pooled, grads, grad_proj)
+    return (pooled, grad_a.T, grad_b.T, proj_grad_a, proj_grad_b)
 
 
 def solution(mesh):

time: 92.9 us -> 74.9 us (0.81)
  local copies, waits for them, and re-layouts: 10.9 us -> 0 us
  Pallas kernels: 80.8 us -> 74.1 us
    pallas_call x1, Pallas kernels: 80.8 us -> 72.1 us  [body(): pl.pallas_call(functools.partial(kernel, shards, replicas), out_shape=(ja...]
    unnamed x23 -> x0, local copies, waits for them, and re-layouts: 8.3 us -> none
    slice x4 -> x0, local copies, waits for them, and re-layouts: 2.64 us -> none  [the longest x1 0.72 us: body(): grads[:, :wide_a]]
    pallas_call x0 -> x1, Pallas kernels: none -> 1.95 us  [body(): pl.pallas_call(finish, out_shape=(jax.ShapeDtypeStruct((bags, embed), BF1...]
where the time goes in v3:
time: 74.9 us; the launch traced here: 74.7 us
  Pallas kernels  74.1 us (99%)
    pallas_call x1, Pallas kernels, body(): pl.pallas_call(functools.partial(kernel, shards, replicas), out_shape=(ja...  72.1 us
    pallas_call x1, Pallas kernels, body(): pl.pallas_call(finish, out_shape=(jax.ShapeDtypeStruct((bags, embed), BF1...  1.95 us

profile of v3, /device:TPU:1, one launch (start us, length us, event | category | flops | bytes accessed | tf_op | source)
XLA Modules:
  0.0 74.7 jit_solution(9613652407384862816)
XLA Ops:
  0.6 72.1 %shard_map.146 = (bf16[512,256]{1,0:T(8,128)(2,1)}, bf16[96,1024]{1,0:T(8,128)(2,1)}, f32[96,256]{1,0:T(8,128)}) custom-call(bf16[64,1024]{1,0:T(8,128)(2,1)} %bitcast.8, bf16[32,1024]{1,0:T(8,128)(2,1)} %bitcast.9, bf16[64,256]{1,0:T(8,128)(2,1)} %proj_a.1, bf16[32,256]{1,0:T(8,128)(2,1)} %proj_b.1, s32[1,1024]{1,0:T(1,128)} %bitcast.10, ...), custom_call_target="tpu_custom_call" | custom-call | tf_op jit(solution)/shard_map/pallas_call | solution.py:362
  72.8 2.0 %shard_map.147 = (bf16[512,256]{1,0:T(8,128)(2,1)}, f32[64,1024]{1,0:T(8,128)}, f32[32,1024]{1,0:T(8,128)}, f32[64,256]{1,0:T(8,128)}, f32[32,256]{1,0:T(8,128)}) custom-call(bf16[512,256]{1,0:T(8,128)(2,1)} %get-tuple-element.13.pooled, bf16[96,1024]{1,0:T(8,128)(2,1)} %get-tuple-element.14.grads, f32[96,256]{1,0:T(8,128)} %get-tuple-element.15.grad_proj), custom_call_target="tpu_custom_call" | custom-call | tf_op jit(solution)/shard_map/pallas_call | solution.py:423

commit v4 on v3

--- a/solution.py
+++ b/solution.py
@@ -9,6 +9,7 @@
 
 F32, BF16, I32 = jnp.float32, jnp.bfloat16, jnp.int32
 LANES = 128
+TILE = 16
 SLOT_ROWS = 24
 GROUPS = 8
 DIGIT = 5
@@ -43,20 +44,20 @@
     return jnp.sum(block * weight, axis=1, keepdims=True).astype(I32)
 
 
-def order(step, start):
+def order(step, start, count):
     odd = step % 2
-    return (start + 4 + (1 - odd) * (step // 2) - odd * ((step + 1) // 2) + GROUPS) % GROUPS
+    return (start + count // 2 + (1 - odd) * (step // 2) - odd * ((step + 1) // 2) + count) % count
 
 
 def kernel(
     shards,
     replicas,
     tab_a, tab_b, proj_a, proj_b, owner_a_in, row_a_in, bag_a_in, owner_b_in, row_b_in, bag_b_in, d_pooled_in,
-    pooled_out, grads_out, proj_out,
+    pooled_to, grads_to, proj_out,
     owner_a, row_a, bag_a, owner_b, row_b, bag_b, d_pooled,
     tabs, proj, slot, give, sent, came, found, back, bags_a, bags_b, grads, looked,
     piece, piece_in, share, share_in, part, part_in, tile, tile_in, done, done_in,
-    in_sems, send_sems, came_sems, back_sems, recv_sems,
+    pooled_out, grads_out, out_sems, in_sems, send_sems, came_sems, back_sems, recv_sems,
 ):
     me, rep = lax.axis_index("shard"), lax.axis_index("rep")
     lookups, rows, bags = owner_a.shape[1], tab_a.shape[1], d_pooled.shape[0]
@@ -65,7 +66,7 @@
     per_group = shards // GROUPS
     slots = per_group * SLOT_ROWS
     my_group = me // per_group
-    holders, per = part.shape[0], part.shape[1] // 8
+    holders, per = part.shape[0], part.shape[1] // TILE
     stride = shards // holders
 
     loads = [
@@ -90,16 +91,36 @@
         load.start()
     barrier = pltpu.get_barrier_semaphore()
 
-    def greet_shard(step, carry):
-        pl.semaphore_signal(barrier, inc=1, device_id=((me + step) % shards, rep), device_id_type=pl.DeviceIdType.MESH)
-        return carry
-
-    def greet_rep(step, carry):
-        pl.semaphore_signal(barrier, inc=1, device_id=(me, (rep + step) % replicas), device_id_type=pl.DeviceIdType.MESH)
-        return carry
-
-    lax.fori_loop(1, shards, greet_shard, 0)
-    lax.fori_loop(1, replicas, greet_rep, 0)
+    def each_rep(visit):
+        def one(step, carry):
+            visit(order(step, rep, replicas))
+            return carry
+
+        lax.fori_loop(0, replicas - 1, one, 0)
+
+    def each_shard(visit):
+        def group_of(step, carry):
+            first = order(step, my_group, GROUPS) * per_group
+
+            def one(i, inner):
+                visit(first + i)
+                return inner
+
+            return lax.fori_loop(0, per_group, one, carry)
+
+        lax.fori_loop(0, GROUPS - 1, group_of, 0)
+
+        def beside(i, carry):
+            visit(my_group * per_group + (me + i) % per_group)
+            return carry
+
+        lax.fori_loop(1, per_group, beside, 0)
+
+    def greet(*target):
+        pl.semaphore_signal(barrier, inc=1, device_id=target, device_id_type=pl.DeviceIdType.MESH)
+
+    each_rep(lambda target: greet(me, target))
+    each_shard(lambda target: greet(target, rep))
 
     proj[wide:, :] = jnp.zeros((LANES - wide, proj.shape[1]), BF16)
     tabs[0, wide_a:, :] = jnp.zeros((LANES - wide_a, rows), BF16)
@@ -173,7 +194,7 @@
         lax.fori_loop(0, per_group, one, 0)
 
     def ask(step, carry):
-        group = order(step, my_group)
+        group = order(step, my_group, GROUPS)
         at = iota((slots, lookups), 0) + group * slots
         block = dot(onehot(slot[0:1, :] == at), give[0], ((1,), (1,)))
         block += dot(onehot(slot[1:2, :] == at), give[1], ((1,), (1,)))
@@ -190,7 +211,7 @@
         load.wait()
 
     def answer(step, carry):
-        group = order(step, my_group)
+        group = order(step, my_group, GROUPS)
         mine = pl.ds(group * per_group, per_group)
         wait_bytes(came.at[mine], came_sems.at[group])
         block = came[mine].astype(F32).reshape(slots, LANES)
@@ -214,12 +235,7 @@
         piece[k] = grads[high : high + tall, left : left + broad].astype(BF16)
     piece_in[rep] = piece[rep]
 
-    def scatter(step, carry):
-        target = (rep + step) % replicas
-        to_rep(piece.at[target], piece_in.at[rep], target, send_sems.at[2], recv_sems.at[0])
-        return carry
-
-    lax.fori_loop(1, replicas, scatter, 0)
+    each_rep(lambda target: to_rep(piece.at[target], piece_in.at[rep], target, send_sems.at[2], recv_sems.at[0]))
 
     def mark(group, carry):
         block = sent[pl.ds(group * per_group, per_group)].astype(F32).reshape(slots, LANES)
@@ -231,7 +247,7 @@
     lax.fori_loop(0, GROUPS, mark, 0)
 
     def pool(step, carry):
-        group = order(step, my_group)
+        group = order(step, my_group, GROUPS)
         mine = pl.ds(group * per_group, per_group)
         wait_bytes(back.at[mine], back_sems.at[group])
         turned = back[mine].astype(F32).reshape(slots, LANES).T.astype(BF16)
@@ -248,8 +264,9 @@
     embed = partial.shape[1]
     halves = embed // LANES
     for k in range(holders * per):
-        top, left = (k // halves) * 8, (k % halves) * LANES
-        part[k // per, (k % per) * 8 : (k % per) * 8 + 8, :] = partial[top : top + 8, left : left + LANES]
+        top, left = (k // halves) * TILE, (k % halves) * LANES
+        first = (k % per) * TILE
+        part[k // per, first : first + TILE, :] = partial[top : top + TILE, left : left + LANES].astype(BF16)
     index = me // stride
     holding = jnp.logical_and(me == index * stride, index < holders)
 
@@ -268,47 +285,37 @@
     def _():
         part_in[me] = part[index]
         wait_bytes(part_in.at[pl.ds(0, shards - 1)], recv_sems.at[2])
-        tile[...] = jnp.sum(part_in[...], axis=0)
+        tile[...] = jnp.sum(part_in[...].astype(F32), axis=0).astype(BF16)
         tile_in[rep] = tile[...]
-
-        def swap(step, carry):
-            to_rep(tile, tile_in.at[rep], (rep + step) % replicas, send_sems.at[5], recv_sems.at[3])
-            return carry
-
-        lax.fori_loop(1, replicas, swap, 0)
+        each_rep(lambda target: to_rep(tile, tile_in.at[rep], target, send_sems.at[5], recv_sems.at[3]))
 
     wait_bytes(piece_in.at[pl.ds(0, replicas - 1)], recv_sems.at[0])
     share[...] = jnp.sum(piece_in[...].astype(F32), axis=0).astype(BF16)
     share_in[rep] = share[...]
 
-    def give_share(step, carry):
-        to_rep(share, share_in.at[rep], (rep + step) % replicas, send_sems.at[3], recv_sems.at[1])
-        return carry
-
-    lax.fori_loop(1, replicas, give_share, 0)
+    each_rep(lambda target: to_rep(share, share_in.at[rep], target, send_sems.at[3], recv_sems.at[1]))
 
     @pl.when(holding)
     def _():
         wait_bytes(tile_in.at[pl.ds(0, replicas - 1)], recv_sems.at[3])
         scale = 1.0 / (float(lookups * shards * replicas) ** 0.5)
-        done[...] = jnp.sum(tile_in[...], axis=0) * scale
+        done[...] = (jnp.sum(tile_in[...].astype(F32), axis=0) * scale).astype(BF16)
         done_in[index] = done[...]
-
-        def tell(step, carry):
-            to_shard(done, done_in.at[index], (me + step) % shards, send_sems.at[6], recv_sems.at[4])
-            return carry
-
-        lax.fori_loop(1, shards, tell, 0)
+        each_shard(lambda target: to_shard(done, done_in.at[index], target, send_sems.at[6], recv_sems.at[4]))
 
     turned = looked[...].T
     high = turned.astype(BF16)
     low = (turned - high.astype(F32)).astype(BF16)
     pooled_out[...] = (dot(high, proj[...]) + dot(low, proj[...])).astype(BF16)
+    store_pooled = pltpu.make_async_copy(pooled_out, pooled_to, out_sems.at[0])
+    store_pooled.start()
 
     wait_bytes(share_in.at[pl.ds(0, replicas - 1)], recv_sems.at[1])
     for k in range(replicas):
         top, left = (k // across) * tall, (k % across) * broad
         grads_out[top : top + tall, left : left + broad] = share_in[k]
+    store_grads = pltpu.make_async_copy(grads_out, grads_to, out_sems.at[1])
+    store_grads.start()
 
     @pl.when(holding)
     def _():
@@ -319,9 +326,12 @@
         wait_bytes(done_in, recv_sems.at[4])
 
     for k in range(holders * per):
-        top, left = (k // halves) * 8, (k % halves) * LANES
-        proj_out[top : top + 8, left : left + LANES] = done_in[k // per, (k % per) * 8 : (k % per) * 8 + 8, :]
-
+        top, left = (k // halves) * TILE, (k % halves) * LANES
+        first = (k % per) * TILE
+        proj_out[top : top + TILE, left : left + LANES] = done_in[k // per, first : first + TILE, :].astype(F32)
+
+    store_pooled.wait()
+    store_grads.wait()
     wait_bytes(sent.at[pl.ds(0, shards - 1)], send_sems.at[0])
     wait_bytes(found.at[pl.ds(0, shards - 1)], send_sems.at[1])
     wait_bytes(piece.at[pl.ds(0, replicas - 1)], send_sems.at[2])
@@ -353,8 +363,8 @@
     rows, wide_a = table_a.shape
     wide = wide_a + table_b.shape[1]
     bags, embed = d_pooled.shape
-    tiles = wide * embed // (8 * LANES)
-    holders = min(tiles, shards)
+    tiles = wide * embed // (TILE * LANES)
+    holders = max(h for h in range(1, min(tiles, shards) + 1) if tiles % h == 0)
     per = tiles // holders
     tall, broad = wide // 2, 2 * rows // replicas
     block = pltpu.VMEM((shards, SLOT_ROWS, LANES), BF16)
@@ -367,7 +377,11 @@
             jax.ShapeDtypeStruct((wide, embed), F32),
         ),
         in_specs=[pl.BlockSpec(memory_space=pltpu.HBM)] * 11,
-        out_specs=(pl.BlockSpec(memory_space=pltpu.VMEM),) * 3,
+        out_specs=(
+            pl.BlockSpec(memory_space=pltpu.HBM),
+            pl.BlockSpec(memory_space=pltpu.HBM),
+            pl.BlockSpec(memory_space=pltpu.VMEM),
+        ),
         scratch_shapes=[
             pltpu.VMEM(line, I32),
             pltpu.VMEM(line, I32),
@@ -392,12 +406,15 @@
             pltpu.VMEM((replicas, tall, broad), BF16),
             pltpu.VMEM((tall, broad), BF16),
             pltpu.VMEM((replicas, tall, broad), BF16),
-            pltpu.VMEM((holders, 8 * per, LANES), F32),
-            pltpu.VMEM((shards, 8 * per, LANES), F32),
-            pltpu.VMEM((8 * per, LANES), F32),
-            pltpu.VMEM((replicas, 8 * per, LANES), F32),
-            pltpu.VMEM((8 * per, LANES), F32),
-            pltpu.VMEM((holders, 8 * per, LANES), F32),
+            pltpu.VMEM((holders, TILE * per, LANES), BF16),
+            pltpu.VMEM((shards, TILE * per, LANES), BF16),
+            pltpu.VMEM((TILE * per, LANES), BF16),
+            pltpu.VMEM((replicas, TILE * per, LANES), BF16),
+            pltpu.VMEM((TILE * per, LANES), BF16),
+            pltpu.VMEM((holders, TILE * per, LANES), BF16),
+            pltpu.VMEM((bags, embed), BF16),
+            pltpu.VMEM((wide, rows), BF16),
+            pltpu.SemaphoreType.DMA((2,)),
             pltpu.SemaphoreType.DMA((11,)),
             pltpu.SemaphoreType.DMA((7,)),
             pltpu.SemaphoreType.DMA((GROUPS,)),

time: 74.9 us -> 70.2 us (0.937)
  Pallas kernels: 74.1 us -> 69.4 us
    pallas_call x1, Pallas kernels: 72.1 us -> 67.4 us  [body(): pl.pallas_call(functools.partial(kernel, shards, replicas), out_shape=(ja...]
where the time goes in v4:
time: 70.2 us; the launch traced here: 70 us
  Pallas kernels  69.4 us (99%)
    pallas_call x1, Pallas kernels, body(): pl.pallas_call(functools.partial(kernel, shards, replicas), out_shape=(ja...  67.4 us
    pallas_call x1, Pallas kernels, body(): pl.pallas_call(finish, out_shape=(jax.ShapeDtypeStruct((bags, embed), BF1...  1.95 us

profile of v4, /device:TPU:1, one launch (start us, length us, event | category | flops | bytes accessed | tf_op | source)
XLA Modules:
  0.0 70.0 jit_solution(6642764397714125912)
XLA Ops:
  0.6 67.4 %shard_map.146 = (bf16[512,256]{1,0:T(8,128)(2,1)}, bf16[96,1024]{1,0:T(8,128)(2,1)}, f32[96,256]{1,0:T(8,128)}) custom-call(bf16[64,1024]{1,0:T(8,128)(2,1)} %bitcast.8, bf16[32,1024]{1,0:T(8,128)(2,1)} %bitcast.9, bf16[64,256]{1,0:T(8,128)(2,1)} %proj_a.1, bf16[32,256]{1,0:T(8,128)(2,1)} %proj_b.1, s32[1,1024]{1,0:T(1,128)} %bitcast.10, ...), custom_call_target="tpu_custom_call" | custom-call | tf_op jit(solution)/shard_map/pallas_call | solution.py:372
  68.0 2.0 %shard_map.147 = (bf16[512,256]{1,0:T(8,128)(2,1)}, f32[64,1024]{1,0:T(8,128)}, f32[32,1024]{1,0:T(8,128)}, f32[64,256]{1,0:T(8,128)}, f32[32,256]{1,0:T(8,128)}) custom-call(bf16[512,256]{1,0:T(8,128)(2,1)} %get-tuple-element.13.pooled, bf16[96,1024]{1,0:T(8,128)(2,1)} %get-tuple-element.14.grads, f32[96,256]{1,0:T(8,128)} %get-tuple-element.15.grad_proj), custom_call_target="tpu_custom_call" | custom-call | tf_op jit(solution)/shard_map/pallas_call | solution.py:440

commit v5 on v4

--- a/solution.py
+++ b/solution.py
@@ -13,7 +13,7 @@
 SLOT_ROWS = 24
 GROUPS = 8
 DIGIT = 5
-VMEM = 64 * 1024 * 1024
+LIMIT, SMALL = 48 * 1024 * 1024, 16 * 1024 * 1024
 
 
 def dot(left, right, dims=((1,), (0,))):
@@ -53,11 +53,11 @@
     shards,
     replicas,
     tab_a, tab_b, proj_a, proj_b, owner_a_in, row_a_in, bag_a_in, owner_b_in, row_b_in, bag_b_in, d_pooled_in,
-    pooled_to, grads_to, proj_out,
+    pooled_out, grads_out, proj_out,
     owner_a, row_a, bag_a, owner_b, row_b, bag_b, d_pooled,
     tabs, proj, slot, give, sent, came, found, back, bags_a, bags_b, grads, looked,
     piece, piece_in, share, share_in, part, part_in, tile, tile_in, done, done_in,
-    pooled_out, grads_out, out_sems, in_sems, send_sems, came_sems, back_sems, recv_sems,
+    in_sems, send_sems, came_sems, back_sems, recv_sems,
 ):
     me, rep = lax.axis_index("shard"), lax.axis_index("rep")
     lookups, rows, bags = owner_a.shape[1], tab_a.shape[1], d_pooled.shape[0]
@@ -307,15 +307,11 @@
     high = turned.astype(BF16)
     low = (turned - high.astype(F32)).astype(BF16)
     pooled_out[...] = (dot(high, proj[...]) + dot(low, proj[...])).astype(BF16)
-    store_pooled = pltpu.make_async_copy(pooled_out, pooled_to, out_sems.at[0])
-    store_pooled.start()
 
     wait_bytes(share_in.at[pl.ds(0, replicas - 1)], recv_sems.at[1])
     for k in range(replicas):
         top, left = (k // across) * tall, (k % across) * broad
         grads_out[top : top + tall, left : left + broad] = share_in[k]
-    store_grads = pltpu.make_async_copy(grads_out, grads_to, out_sems.at[1])
-    store_grads.start()
 
     @pl.when(holding)
     def _():
@@ -330,8 +326,6 @@
         first = (k % per) * TILE
         proj_out[top : top + TILE, left : left + LANES] = done_in[k // per, first : first + TILE, :].astype(F32)
 
-    store_pooled.wait()
-    store_grads.wait()
     wait_bytes(sent.at[pl.ds(0, shards - 1)], send_sems.at[0])
     wait_bytes(found.at[pl.ds(0, shards - 1)], send_sems.at[1])
     wait_bytes(piece.at[pl.ds(0, replicas - 1)], send_sems.at[2])
@@ -377,11 +371,7 @@
             jax.ShapeDtypeStruct((wide, embed), F32),
         ),
         in_specs=[pl.BlockSpec(memory_space=pltpu.HBM)] * 11,
-        out_specs=(
-            pl.BlockSpec(memory_space=pltpu.HBM),
-            pl.BlockSpec(memory_space=pltpu.HBM),
-            pl.BlockSpec(memory_space=pltpu.VMEM),
-        ),
+        out_specs=(pl.BlockSpec(memory_space=pltpu.VMEM),) * 3,
         scratch_shapes=[
             pltpu.VMEM(line, I32),
             pltpu.VMEM(line, I32),
@@ -412,9 +402,6 @@
             pltpu.VMEM((replicas, TILE * per, LANES), BF16),
             pltpu.VMEM((TILE * per, LANES), BF16),
             pltpu.VMEM((holders, TILE * per, LANES), BF16),
-            pltpu.VMEM((bags, embed), BF16),
-            pltpu.VMEM((wide, rows), BF16),
-            pltpu.SemaphoreType.DMA((2,)),
             pltpu.SemaphoreType.DMA((11,)),
             pltpu.SemaphoreType.DMA((7,)),
             pltpu.SemaphoreType.DMA((GROUPS,)),
@@ -422,20 +409,25 @@
             pltpu.SemaphoreType.DMA((5,)),
         ],
         compiler_params=pltpu.CompilerParams(
-            collective_id=0, has_side_effects=True, vmem_limit_bytes=VMEM
+            collective_id=0, has_side_effects=True, vmem_limit_bytes=LIMIT
         ),
     )(
-        table_a.T,
-        table_b.T,
-        proj_a,
-        proj_b,
-        owner_a.reshape(line),
-        row_a.reshape(line),
-        bag_a,
-        owner_b.reshape(line),
-        row_b.reshape(line),
-        bag_b,
-        d_pooled,
+        *(
+            pltpu.with_memory_space_constraint(x, pltpu.HBM)
+            for x in (
+                table_a.T,
+                table_b.T,
+                proj_a,
+                proj_b,
+                owner_a.reshape(line),
+                row_a.reshape(line),
+                bag_a,
+                owner_b.reshape(line),
+                row_b.reshape(line),
+                bag_b,
+                d_pooled,
+            )
+        )
     )
     pooled, grad_a, grad_b, proj_grad_a, proj_grad_b = pl.pallas_call(
         finish,
@@ -448,7 +440,7 @@
         ),
         in_specs=[pl.BlockSpec(memory_space=pltpu.VMEM)] * 3,
         out_specs=(pl.BlockSpec(memory_space=pltpu.VMEM),) * 5,
-        compiler_params=pltpu.CompilerParams(vmem_limit_bytes=VMEM),
+        compiler_params=pltpu.CompilerParams(vmem_limit_bytes=SMALL),
     )(pooled, grads, grad_proj)
     return (pooled, grad_a.T, grad_b.T, proj_grad_a, proj_grad_b)
 

time: 70.2 us -> 68.4 us (0.974)
  Pallas kernels: 69.4 us -> 67.7 us
    pallas_call x1, Pallas kernels: 1.95 us -> 0.9 us  [body(): pl.pallas_call(finish, out_shape=(jax.ShapeDtypeStruct((bags, embed), BF1...]
where the time goes in v5:
time: 68.4 us; the launch traced here: 68.3 us
  Pallas kernels  67.7 us (99%)
    pallas_call x1, Pallas kernels, body(): pl.pallas_call(functools.partial(kernel, shards, replicas), out_shape=(ja...  66.8 us

profile of v5, /device:TPU:1, one launch (start us, length us, event | category | flops | bytes accessed | tf_op | source)
XLA Modules:
  0.0 68.3 jit_solution(7227968481564599149)
XLA Ops:
  0.6 66.8 %shard_map.146 = (bf16[512,256]{1,0:T(8,128)(2,1)S(1)}, bf16[96,1024]{1,0:T(8,128)(2,1)S(1)}, f32[96,256]{1,0:T(8,128)S(1)}) custom-call(bf16[64,1024]{1,0:T(8,128)(2,1)} %bitcast.8, bf16[32,1024]{1,0:T(8,128)(2,1)} %bitcast.9, bf16[64,256]{1,0:T(8,128)(2,1)} %proj_a.1, bf16[32,256]{1,0:T(8,128)(2,1)} %proj_b.1, s32[1,1024]{1,0:T(1,128)} %bitcast.10, ...), custom_call_target="tpu_custom_call" | custom-call | tf_op jit(solution)/shard_map/pallas_call | solution.py:366
  67.4 0.9 %shard_map.147 = (bf16[512,256]{1,0:T(8,128)(2,1)}, f32[64,1024]{1,0:T(8,128)}, f32[32,1024]{1,0:T(8,128)}, f32[64,256]{1,0:T(8,128)}, f32[32,256]{1,0:T(8,128)}) custom-call(bf16[512,256]{1,0:T(8,128)(2,1)S(1)} %get-tuple-element.13.pooled, bf16[96,1024]{1,0:T(8,128)(2,1)S(1)} %get-tuple-element.14.grads, f32[96,256]{1,0:T(8,128)S(1)} %get-tuple-element.15.grad_proj), custom_call_target="tpu_custom_call" | custom-call | tf_op jit(solution)/shard_map/pallas_call | solution.py:432

commit v6 on v5

--- a/solution.py
+++ b/solution.py
@@ -155,6 +155,14 @@
         give[0, wide:, cut] = (digits(row_a[:, cut], 0, tail) + digits(bag_a[:, cut] + 1, 2, tail)).astype(F32).astype(BF16)
         give[1, wide:, cut] = (digits(row_b[:, cut], 4, tail) + digits(bag_b[:, cut] + 1, 6, tail)).astype(F32).astype(BF16)
 
+    def fill(step):
+        group = order(step, my_group, GROUPS)
+        at = iota((slots, lookups), 0) + group * slots
+        block = dot(onehot(slot[0:1, :] == at), give[0], ((1,), (1,)))
+        block += dot(onehot(slot[1:2, :] == at), give[1], ((1,), (1,)))
+        sent[pl.ds(group * per_group, per_group)] = block.reshape(per_group, SLOT_ROWS, LANES).astype(BF16)
+
+    fill(0)
     pl.semaphore_wait(barrier, shards + replicas - 2)
 
     def to_shard(block, there, target, send_sem, recv_sem):
@@ -194,15 +202,12 @@
         lax.fori_loop(0, per_group, one, 0)
 
     def ask(step, carry):
-        group = order(step, my_group, GROUPS)
-        at = iota((slots, lookups), 0) + group * slots
-        block = dot(onehot(slot[0:1, :] == at), give[0], ((1,), (1,)))
-        block += dot(onehot(slot[1:2, :] == at), give[1], ((1,), (1,)))
-        sent[pl.ds(group * per_group, per_group)] = block.reshape(per_group, SLOT_ROWS, LANES).astype(BF16)
-        send_group(group, sent, came, send_sems.at[0], came_sems.at[my_group])
+        send_group(order(step, my_group, GROUPS), sent, came, send_sems.at[0], came_sems.at[my_group])
+        fill(step + 1)
         return carry
 
-    lax.fori_loop(0, GROUPS, ask, 0)
+    lax.fori_loop(0, GROUPS - 1, ask, 0)
+    send_group(order(GROUPS - 1, my_group, GROUPS), sent, came, send_sems.at[0], came_sems.at[my_group])
 
     grads[...] = jnp.zeros_like(grads)
     looked[...] = jnp.zeros_like(looked)

time: 68.4 us -> 68.6 us (level)
  no operation moved by 1% of the time
where the time goes in v6:
time: 68.6 us; the launch traced here: 68.5 us
  Pallas kernels  67.9 us (99%)
    pallas_call x1, Pallas kernels, body(): pl.pallas_call(functools.partial(kernel, shards, replicas), out_shape=(ja...  67 us

profile of v6, /device:TPU:1, one launch (start us, length us, event | category | flops | bytes accessed | tf_op | source)
XLA Modules:
  0.0 68.5 jit_solution(15593760532359218558)
XLA Ops:
  0.6 67.0 %shard_map.146 = (bf16[512,256]{1,0:T(8,128)(2,1)S(1)}, bf16[96,1024]{1,0:T(8,128)(2,1)S(1)}, f32[96,256]{1,0:T(8,128)S(1)}) custom-call(bf16[64,1024]{1,0:T(8,128)(2,1)} %bitcast.8, bf16[32,1024]{1,0:T(8,128)(2,1)} %bitcast.9, bf16[64,256]{1,0:T(8,128)(2,1)} %proj_a.1, bf16[32,256]{1,0:T(8,128)(2,1)} %proj_b.1, s32[1,1024]{1,0:T(1,128)} %bitcast.10, ...), custom_call_target="tpu_custom_call" | custom-call | tf_op jit(solution)/shard_map/pallas_call | solution.py:371
  67.6 0.9 %shard_map.147 = (bf16[512,256]{1,0:T(8,128)(2,1)}, f32[64,1024]{1,0:T(8,128)}, f32[32,1024]{1,0:T(8,128)}, f32[64,256]{1,0:T(8,128)}, f32[32,256]{1,0:T(8,128)}) custom-call(bf16[512,256]{1,0:T(8,128)(2,1)S(1)} %get-tuple-element.13.pooled, bf16[96,1024]{1,0:T(8,128)(2,1)S(1)} %get-tuple-element.14.grads, f32[96,256]{1,0:T(8,128)S(1)} %get-tuple-element.15.grad_proj), custom_call_target="tpu_custom_call" | custom-call | tf_op jit(solution)/shard_map/pallas_call | solution.py:437
